TPU v7x, 32 devices: a whole 2x2x4 slice. The times are simulated.
32 devices in a mesh: fsdp: 16 (over z, x, core), tp: 2 (over y).
Axes of the slice: x: 2, y: 2, z: 4, core: 2. Of those that a mesh axis runs over, the one named last changes fastest.
Arguments:
- hidden: bfloat16 [1024, 26624], P('fsdp', 'tp'), may hold values from -6 to 6
- out_grad: bfloat16 [1024, 16384], P('tp', 'fsdp'), may hold values from -6 to 6
- weight: bfloat16 [26624, 16384], P('tp', 'fsdp'), may hold values from -0.0390625 to 0.0390625
Outputs:
- hidden_grad: bfloat16 [1024, 26624], P('fsdp', 'tp')
- weight_grad: float32 [26624, 16384], P('tp', 'fsdp')
All inputs are finite; a program needn't handle non-finite values.
Results may differ from a plain program's by a relative error of at most 0.015.
Values may be sent and summed in bfloat16 or wider, within the bound.
A program may use at most 192 MiB of HBM per device.

v0:
```python
import math

import jax
import jax.numpy as jnp
from jax import lax
from jax.sharding import PartitionSpec as P


def local(hidden, out_grad, weight):
    grad_rows = lax.all_gather(out_grad, "tp", axis=0, tiled=True)
    partial_sum = lax.dot_general(
        grad_rows, weight, (((1,), (1,)), ((), ())), preferred_element_type=jnp.float32
    )
    adjoint = lax.psum_scatter(
        partial_sum.astype(jnp.bfloat16), "fsdp", scatter_dimension=0, tiled=True
    ).astype(jnp.float32)
    hidden_grad = (adjoint + 0.5 * hidden.astype(jnp.float32)).astype(jnp.bfloat16)
    all_hidden = lax.all_gather(hidden, "fsdp", axis=0, tiled=True)
    weight_grad = lax.dot_general(
        all_hidden, grad_rows, (((0,), (0,)), ((), ())), preferred_element_type=jnp.float32
    )
    grad_scale = 1.0 / math.sqrt(grad_rows.shape[0])
    return (hidden_grad, weight_grad * grad_scale)


def solution(mesh):
    placed = (P("fsdp", "tp"), P("tp", "fsdp"), P("tp", "fsdp"))
    return jax.shard_map(
        local,
        mesh=mesh,
        in_specs=placed,
        out_specs=(P("fsdp", "tp"), P("tp", "fsdp")),
        check_vma=False,
    )
```

profile of v0, /device:TPU:0, one launch (start us, length us, event | category | flops | bytes accessed | tf_op | source)
XLA Modules:
  0.0 525.9 jit_solution(13764649302727604620)
XLA Ops:
  7.2 0.0 all-gather.3.cloned.1.call-start
  7.2 0.7 all-gather.3.cloned.1.call-update
  7.9 0.0 reduce-scatter.2.cloned.1.call-start
  7.9 37.5 %all-gather.3.cloned.1.call-done = bf16[1024,1024]{1,0:T(8,128)(2,1)} async-done(((bf16[512,1024]{1,0:T(8,128)(2,1)}), bf16[1024,1024]{1,0:T(8,128)(2,1)}) %all-gather.3.cloned.1.call-update) | async-done | bytes 2097168 | tf_op jit(solution)/shard_map/all_gather | solution.py:10
  45.4 35.4 %convolution_convert_fusion = bf16[1024,13312]{1,0:T(8,128)(2,1)} fusion(bf16[1024,1024]{1,0:T(8,128)(2,1)} %all-gather.3.cloned.1.call-done, bf16[13312,1024]{1,0:T(8,128)(2,1)} %param.5), kind=kOutput, calls=%fused_computation.1 | convolution fusion | flops 27930918912 | bytes 56623104 | tf_op jit(solution)/shard_map/dot_general | solution.py:11
  80.8 0.0 copy-start
  80.8 0.0 reduce-scatter.2.cloned.1.call-update
  80.8 0.2 all-gather.5.cloned.1.call-start
  81.1 0.5 all-gather.5.cloned.1.call-update
  81.6 260.2 %reduce-scatter.2.cloned.1.call-done = bf16[64,13312]{1,0:T(8,128)(2,1)} async-done(((bf16[1024,13312]{1,0:T(8,128)(2,1)}), bf16[64,13312]{1,0:T(8,128)(2,1)}) %reduce-scatter.2.cloned.1.call-update) | async-done | bytes 1703952 | tf_op jit(solution)/shard_map/reduce_scatter | solution.py:14
  341.7 0.0 copy-done
  341.7 3.1 add_convert_fusion
  344.9 136.1 %all-gather.5.cloned.1.call-done = bf16[1024,13312]{1,0:T(8,128)(2,1)} async-done(((bf16[64,13312]{1,0:T(8,128)(2,1)}), bf16[1024,13312]{1,0:T(8,128)(2,1)}) %all-gather.5.cloned.1.call-update) | async-done | bytes 27262992 | tf_op jit(solution)/shard_map/all_gather | solution.py:18
  481.0 38.4 %convolution_multiply_fusion = f32[13312,1024]{1,0:T(8,128)} fusion(bf16[1024,13312]{1,0:T(8,128)(2,1)} %all-gather.5.cloned.1.call-done, bf16[1024,1024]{1,0:T(8,128)(2,1)} %all-gather.3.cloned.1.call-done), kind=kOutput, calls=%fused_computation | convolution fusion | flops 27930918912 | bytes 83886080 | tf_op jit(solution)/shard_map/dot_general | solution.py:19
Async XLA Ops:
  7.2 38.2 %all-gather.3.cloned.1.call-start = ((), (), s32[]{:S(2)}) async-start(), calls=%async_computation.1 | async-start | bytes 3145728 | tf_op jit(solution)/shard_map/all_gather | solution.py:10
  7.9 333.8 %reduce-scatter.2.cloned.1.call-start = ((), (), s32[]{:S(2)}) async-start(), calls=%async_computation.2 | async-start | bytes 28966912 | tf_op jit(solution)/shard_map/reduce_scatter | solution.py:14
  80.8 260.9 %copy-start = (bf16[64,13312]{1,0:T(8,128)(2,1)S(1)}, bf16[64,13312]{1,0:T(8,128)(2,1)}, u32[]{:S(2)}) copy-start(bf16[64,13312]{1,0:T(8,128)(2,1)} %param.3) | copy-start | bytes 5111812
  80.8 400.1 %all-gather.5.cloned.1.call-start = ((), (), s32[]{:S(2)}) async-start(), calls=%async_computation.3 | async-start | bytes 28966912 | tf_op jit(solution)/shard_map/all_gather | solution.py:18
Sparse Core Ops, SparseCore 0:
  9.5 35.8 all-gather.2
  81.0 260.7 reduce-scatter.1
  343.3 137.5 all-gather.4
where the time goes:
time: 526 us
  waiting for transfers between devices  435 us (83%)
  matrix products  73.9 us (14%)
  between operations  13.7 us (3%)
    reduce_scatter x1, waiting for transfers between devices, local(): lax.psum_scatter(partial_sum.astype(jnp.bfloat16), 'fsdp', scatter_dimens...  260 us
    all_gather x1, waiting for transfers between devices, local(): all_hidden = lax.all_gather(hidden, 'fsdp', axis=0, tiled=True)  136 us
    dot_general x1, matrix products, local(): lax.dot_general(all_hidden, grad_rows, (((0,), (0,)), ((), ())), preferre...  38.4 us
    all_gather x1, waiting for transfers between devices, local(): grad_rows = lax.all_gather(out_grad, 'tp', axis=0, tiled=True)  37.5 us
    dot_general x1, matrix products, local(): lax.dot_general(grad_rows, weight, (((1,), (1,)), ((), ())), preferred_el...  35.4 us
  transfers between devices with their start and end apart: 3, of which 3 were waited for; matrix products, arithmetic and copies ran while one was open for 1% of the time, Pallas kernels for 0%

commit v1 on v0

v1 whole, which is shorter than its diff:
```python
import math

import jax
import jax.numpy as jnp
import numpy as np
from jax import lax
from jax.sharding import PartitionSpec as P

SUB = 2


def ring_of(chips):
    order = list(range(0, chips, 2))
    order += [c for c in range(chips - 1, -1, -1) if c % 2 == 1]
    return order


def local(n, n_tp, hidden, out_grad, weight):
    chips = n // 2
    ring = ring_of(chips)
    place = [0] * chips
    for at, chip in enumerate(ring):
        place[chip] = at
    table = np.zeros((n, 2, chips), np.int32)
    for i in range(n):
        for d, step in enumerate((1, -1)):
            table[i, d] = [ring[(place[i // 2] - step * s) % chips] for s in range(chips)]
    me = lax.axis_index("fsdp")
    core = lax.rem(me, 2)
    behind = lax.dynamic_slice(
        jnp.asarray(table), (me, 0, 0), (1, 2, chips), allow_negative_indices=False
    )

    def chip_behind(step, s):
        return behind[0, 0 if step == 1 else 1, s]

    def put(into, block, at):
        start = (at,) + (0,) * block.ndim
        return lax.dynamic_update_slice(into, block[None], start, allow_negative_indices=False)

    def take(whole, at):
        start = (at,) + (0,) * (whole.ndim - 1)
        return lax.dynamic_slice(
            whole, start, (1,) + whole.shape[1:], allow_negative_indices=False
        )[0]

    def shift(value, step):
        pairs = []
        for i in range(chips):
            for c in range(2):
                pairs.append((ring[i] * 2 + c, ring[(i + step) % chips] * 2 + c))
        return lax.ppermute(value, "fsdp", pairs)

    def swap(value):
        return lax.ppermute(value, "fsdp", [(i, i ^ 1) for i in range(n)])

    rows, width = hidden.shape
    piece = width // (2 * SUB)
    chains = [(k * piece, 1 if k % 2 == 0 else -1) for k in range(2 * SUB)]

    tp_at = lax.axis_index("tp")
    part = out_grad.shape[0]
    grad_rows = jnp.zeros((n_tp,) + out_grad.shape, out_grad.dtype)
    grad_rows = put(grad_rows, out_grad, tp_at)
    for i in range(1, n_tp):
        other = lax.ppermute(out_grad, "tp", [(j, (j + i) % n_tp) for j in range(n_tp)])
        grad_rows = put(grad_rows, other, lax.rem(tp_at - i + n_tp, n_tp))
    grad_rows = grad_rows.reshape(n_tp * part, -1)

    held = [hidden[:, c : c + piece] for c, _ in chains]
    own = list(held)
    gathered = [jnp.zeros((n, rows, piece), hidden.dtype) for _ in chains]
    for k, block in enumerate(held):
        gathered[k] = put(gathered[k], block, me)
        gathered[k] = put(gathered[k], swap(block), me + 1 - 2 * core)
    for s in range(1, chips):
        for k, (_, step) in enumerate(chains):
            held[k] = shift(held[k], step)
            owner = chip_behind(step, s) * 2
            gathered[k] = put(gathered[k], held[k], owner + core)
            gathered[k] = put(gathered[k], swap(held[k]), owner + 1 - core)

    split = grad_rows.reshape(chips, 2, rows, -1).transpose(1, 0, 2, 3)
    nt = (((1,), (1,)), ((), ()))

    def partial(c, k):
        first = chains[k][0]
        mine = take(split, c).reshape(chips * rows, -1)
        out = lax.dot_general(
            mine, weight[first : first + piece], nt, preferred_element_type=jnp.float32
        )
        return out.astype(jnp.bfloat16).reshape(chips, rows, piece)

    theirs = [swap(partial(1 - core, k)) for k in range(len(chains))]
    ours = [partial(core, k) for k in range(len(chains))]

    def term(k, chip):
        return take(ours[k], chip).astype(jnp.float32) + take(theirs[k], chip).astype(jnp.float32)

    sums = []
    for k, (_, step) in enumerate(chains):
        first = term(k, chip_behind(step, 1)).astype(jnp.bfloat16)
        first, held[k] = lax.optimization_barrier((first, held[k]))
        sums.append(first)
    scale = 1.0 / math.sqrt(grad_rows.shape[0])
    weight_grad = jnp.zeros((width, grad_rows.shape[1]), jnp.float32)
    tn = (((0,), (0,)), ((), ()))
    for s in range(1, chips):
        for k, (_, step) in enumerate(chains):
            total = shift(sums[k], step).astype(jnp.float32)
            total = total + term(k, chip_behind(step, (s + 1) % chips))
            if s == chips - 1:
                total = total + 0.5 * own[k].astype(jnp.float32)
            sums[k] = total.astype(jnp.bfloat16)
        if s <= len(chains):
            k = s - 1
            sums[k], block = lax.optimization_barrier((sums[k], gathered[k]))
            block = lax.dot_general(
                block.reshape(n * rows, piece), grad_rows, tn, preferred_element_type=jnp.float32
            )
            weight_grad = lax.dynamic_update_slice(weight_grad, block * scale, (chains[k][0], 0))
    hidden_grad = jnp.concatenate(sums, axis=1)
    return (hidden_grad, weight_grad)


def solution(mesh):
    n, n_tp = mesh.shape["fsdp"], mesh.shape["tp"]
    placed = (P("fsdp", "tp"), P("tp", "fsdp"), P("tp", "fsdp"))
    return jax.shard_map(
        lambda *args: local(n, n_tp, *args),
        mesh=mesh,
        in_specs=placed,
        out_specs=(P("fsdp", "tp"), P("tp", "fsdp")),
        check_vma=False,
    )
```

time: 526 us -> 613 us (1.17)
  waiting for transfers between devices: 435 us -> 281 us
  local copies, waits for them, and re-layouts: 0.01 us -> 78 us
  starting transfers between devices: 0.3 us -> 68.9 us
  other arithmetic: 3.14 us -> 58.5 us
  matrix products: 73.9 us -> 110 us
    ppermute x0 -> x93, waiting for transfers between devices: none -> 281 us  [the longest x56 246 us: shift(): return lax.ppermute(value, 'fsdp', pairs)]
    reduce_scatter x1 -> x0, waiting for transfers between devices: 260 us -> none  [local(): lax.psum_scatter(partial_sum.astype(jnp.bfloat16), 'fsdp', scatter_dimens...]
    all_gather x2 -> x0, waiting for transfers between devices: 174 us -> none  [the longest x1 136 us: local(): all_hidden = lax.all_gather(hidden, 'fsdp', axis=0, tiled=True)]
    ppermute x0 -> x93, starting transfers between devices: none -> 68.9 us  [the longest x56 62.9 us: shift(): return lax.ppermute(value, 'fsdp', pairs)]
    dynamic_update_slice x0 -> x67, local copies, waits for them, and re-layouts: none -> 62.5 us  [the longest x66 41.3 us: put(): lax.dynamic_update_slice(into, block[None], start, allow_negative_indices...]
    convert_element_type x1 -> x29, other arithmetic: 3.14 us -> 57.2 us  [the longest x25 51.6 us: local(): sums[k] = total.astype(jnp.bfloat16)]
    dot_general x2 -> x12, matrix products: 73.9 us -> 110 us  [the longest x8 65.1 us: partial(): lax.dot_general(mine, weight[first:first + piece], nt, preferred_element_...]
  transfers between devices with their start and end apart: 3 -> 93, of which waited for: 3 -> 49; matrix products, arithmetic and copies ran while one was open for 1% -> 39% of each run, Pallas kernels for 0% -> 0%
where the time goes in v1:
time: 613 us; the launch traced here: 607 us
  waiting for transfers between devices  281 us (46%)
  matrix products  110 us (18%)
  local copies, waits for them, and re-layouts  78 us (13%)
  starting transfers between devices  68.9 us (11%)
  other arithmetic  58.5 us (10%)
  between operations  10.4 us (2%)
    ppermute x56, waiting for transfers between devices, shift(): return lax.ppermute(value, 'fsdp', pairs)  246 us
    dot_general x8, matrix products, partial(): lax.dot_general(mine, weight[first:first + piece], nt, preferred_element_...  65.1 us
    ppermute x56, starting transfers between devices, shift(): return lax.ppermute(value, 'fsdp', pairs)  62.9 us
    convert_element_type x25, other arithmetic, local(): sums[k] = total.astype(jnp.bfloat16)  51.6 us
    dot_general x4, matrix products, local(): lax.dot_general(block.reshape(n * rows, piece), grad_rows, tn, preferred_...  44.9 us
    dynamic_update_slice x66, local copies, waits for them, and re-layouts, put(): lax.dynamic_update_slice(into, block[None], start, allow_negative_indices...  41.3 us
    ppermute x36, waiting for transfers between devices, swap(): return lax.ppermute(value, 'fsdp', [(i, i ^ 1) for i in range(n)])  35.3 us
    dynamic_update_slice x1, local copies, waits for them, and re-layouts, local(): lax.dynamic_update_slice(weight_grad, block * scale, (chains[k][0], 0))  21.2 us
  transfers between devices with their start and end apart: 93, of which 49 were waited for; matrix products, arithmetic and copies ran while one was open for 39% of the time, Pallas kernels for 0%

profile of v1, /device:TPU:0, one launch (start us, length us, event | category | flops | bytes accessed | tf_op | source)
XLA Modules:
  0.0 607.2 jit_solution(16320361092683324850)
XLA Ops:
  0.6 2.7 fusion.76
  3.8 2.6 collective-permute-start.2
  9.2 3.9 broadcast.13.clone.1
  15.7 2.2 copy-done.3
  17.9 2.8 copy-done.5
  31.9 2.2 bitcast_dynamic-update-slice_fusion.16
  37.0 15.4 %collective-permute-done.71 = bf16[64,3328]{1,0:T(8,128)(2,1)S(1)} collective-permute-done((bf16[64,3328]{1,0:T(8,128)(2,1)}, bf16[64,3328]{1,0:T(8,128)(2,1)S(1)}, u32[]{:S(2)}, u32[]{:S(2)}) %collective-permute-start.71) | collective-permute-done | bytes 426016 | tf_op jit(solution)/shard_map/ppermute | solution.py:52
  60.4 5.6 collective-permute-done.48
  71.4 17.5 %collective-permute-done.72 = bf16[64,3328]{1,0:T(8,128)(2,1)} collective-permute-done((bf16[64,3328]{1,0:T(8,128)(2,1)S(1)}, bf16[64,3328]{1,0:T(8,128)(2,1)}, u32[]{:S(2)}, u32[]{:S(2)}) %collective-permute-start.72) | collective-permute-done | bytes 426016 | tf_op jit(solution)/shard_map/ppermute | solution.py:52
  92.6 1.8 bitcast_dynamic-update-slice_fusion.45
  96.9 6.5 %collective-permute-done.49 = bf16[64,3328]{1,0:T(8,128)(2,1)S(1)} collective-permute-done((bf16[64,3328]{1,0:T(8,128)(2,1)S(1)}, bf16[64,3328]{1,0:T(8,128)(2,1)S(1)}, u32[]{:S(2)}, u32[]{:S(2)}) %collective-permute-start.49) | collective-permute-done | bytes 426016 | tf_op jit(solution)/shard_map/ppermute | solution.py:52
  106.7 8.5 %fusion.37 = bf16[512,3328]{1,0:T(8,128)(2,1)} fusion(bf16[512,1024]{1,0:T(8,128)(2,1)S(1)} %bitcast.356, bf16[13312,1024]{1,0:T(8,128)(2,1)} %param.6), kind=kOutput, calls=%fused_computation.27 | convolution fusion | flops 3491364864 | bytes 11272192 | tf_op jit(solution)/shard_map/dot_general | solution.py:89
  115.2 8.1 %fusion.31 = bf16[512,3328]{1,0:T(8,128)(2,1)} fusion(bf16[512,1024]{1,0:T(8,128)(2,1)S(1)} %bitcast.357, bf16[13312,1024]{1,0:T(8,128)(2,1)} %param.6), kind=kOutput, calls=%fused_computation.25 | convolution fusion | flops 3491364864 | bytes 11272192 | tf_op jit(solution)/shard_map/dot_general | solution.py:89
  123.3 8.2 %fusion.25 = bf16[512,3328]{1,0:T(8,128)(2,1)} fusion(bf16[512,1024]{1,0:T(8,128)(2,1)S(1)} %bitcast.358, bf16[13312,1024]{1,0:T(8,128)(2,1)} %param.6), kind=kOutput, calls=%fused_computation.23 | convolution fusion | flops 3491364864 | bytes 11272192 | tf_op jit(solution)/shard_map/dot_general | solution.py:89
  131.4 8.1 %fusion.19 = bf16[512,3328]{1,0:T(8,128)(2,1)} fusion(bf16[512,1024]{1,0:T(8,128)(2,1)S(1)} %bitcast.359, bf16[13312,1024]{1,0:T(8,128)(2,1)} %param.6), kind=kOutput, calls=%fused_computation.21 | convolution fusion | flops 3491364864 | bytes 11272192 | tf_op jit(solution)/shard_map/dot_general | solution.py:89
  139.6 6.9 %fusion.34 = bf16[512,3328]{1,0:T(8,128)(2,1)S(1)} fusion(bf16[512,1024]{1,0:T(8,128)(2,1)S(1)} %bitcast.352, bf16[13312,1024]{1,0:T(8,128)(2,1)} %param.6), kind=kOutput, calls=%fused_computation.26 | convolution fusion | flops 3491364864 | bytes 11272192 | tf_op jit(solution)/shard_map/dot_general | solution.py:89
  146.5 6.9 %fusion.28 = bf16[512,3328]{1,0:T(8,128)(2,1)S(1)} fusion(bf16[512,1024]{1,0:T(8,128)(2,1)S(1)} %bitcast.353, bf16[13312,1024]{1,0:T(8,128)(2,1)} %param.6), kind=kOutput, calls=%fused_computation.24 | convolution fusion | flops 3491364864 | bytes 11272192 | tf_op jit(solution)/shard_map/dot_general | solution.py:89
  153.4 9.6 %fusion.22 = bf16[512,3328]{1,0:T(8,128)(2,1)} fusion(bf16[512,1024]{1,0:T(8,128)(2,1)S(1)} %bitcast.354, bf16[13312,1024]{1,0:T(8,128)(2,1)} %param.6), kind=kOutput, calls=%fused_computation.22 | convolution fusion | flops 3491364864 | bytes 11272192 | tf_op jit(solution)/shard_map/dot_general | solution.py:89
  163.0 8.8 %fusion.16 = bf16[512,3328]{1,0:T(8,128)(2,1)} fusion(bf16[512,1024]{1,0:T(8,128)(2,1)} %bitcast.355, bf16[13312,1024]{1,0:T(8,128)(2,1)} %param.6), kind=kOutput, calls=%fused_computation.20 | convolution fusion | flops 3491364864 | bytes 11272192 | tf_op jit(solution)/shard_map/dot_general | solution.py:89
  176.4 7.8 %collective-permute-done.73 = bf16[64,3328]{1,0:T(8,128)(2,1)S(1)} collective-permute-done((bf16[64,3328]{1,0:T(8,128)(2,1)}, bf16[64,3328]{1,0:T(8,128)(2,1)S(1)}, u32[]{:S(2)}, u32[]{:S(2)}) %collective-permute-start.73) | collective-permute-done | bytes 426016 | tf_op jit(solution)/shard_map/ppermute | solution.py:52
  190.7 5.0 collective-permute-done.50
  196.5 6.4 %collective-permute-done.85 = bf16[64,3328]{1,0:T(8,128)(2,1)S(1)} collective-permute-done((bf16[64,3328]{1,0:T(8,128)(2,1)S(1)}, bf16[64,3328]{1,0:T(8,128)(2,1)S(1)}, u32[]{:S(2)}, u32[]{:S(2)}) %collective-permute-start.85) | collective-permute-done | bytes 426016 | tf_op jit(solution)/shard_map/ppermute | solution.py:55
  203.1 4.9 collective-permute-done.37
  209.3 10.6 %collective-permute-done.74 = bf16[64,3328]{1,0:T(8,128)(2,1)S(1)} collective-permute-done((bf16[64,3328]{1,0:T(8,128)(2,1)S(1)}, bf16[64,3328]{1,0:T(8,128)(2,1)S(1)}, u32[]{:S(2)}, u32[]{:S(2)}) %collective-permute-start.74) | collective-permute-done | bytes 426016 | tf_op jit(solution)/shard_map/ppermute | solution.py:52
  220.4 10.7 %collective-permute-done.28 = bf16[64,3328]{1,0:T(8,128)(2,1)S(1)} collective-permute-done((bf16[64,3328]{1,0:T(8,128)(2,1)}, bf16[64,3328]{1,0:T(8,128)(2,1)S(1)}, u32[]{:S(2)}, u32[]{:S(2)}) %collective-permute-start.28) | collective-permute-done | bytes 426016 | tf_op jit(solution)/shard_map/ppermute | solution.py:52
  237.1 9.5 %collective-permute-done.5 = bf16[64,3328]{1,0:T(8,128)(2,1)S(1)} collective-permute-done((bf16[64,3328]{1,0:T(8,128)(2,1)S(1)}, bf16[64,3328]{1,0:T(8,128)(2,1)S(1)}, u32[]{:S(2)}, u32[]{:S(2)}) %collective-permute-start.5) | collective-permute-done | bytes 426016 | tf_op jit(solution)/shard_map/ppermute | solution.py:52
  248.2 9.4 %collective-permute-done.51 = bf16[64,3328]{1,0:T(8,128)(2,1)S(1)} collective-permute-done((bf16[64,3328]{1,0:T(8,128)(2,1)S(1)}, bf16[64,3328]{1,0:T(8,128)(2,1)S(1)}, u32[]{:S(2)}, u32[]{:S(2)}) %collective-permute-start.51) | collective-permute-done | bytes 426016 | tf_op jit(solution)/shard_map/ppermute | solution.py:52
  262.4 10.6 %collective-permute-done.75 = bf16[64,3328]{1,0:T(8,128)(2,1)S(1)} collective-permute-done((bf16[64,3328]{1,0:T(8,128)(2,1)S(1)}, bf16[64,3328]{1,0:T(8,128)(2,1)S(1)}, u32[]{:S(2)}, u32[]{:S(2)}) %collective-permute-start.75) | collective-permute-done | bytes 426016 | tf_op jit(solution)/shard_map/ppermute | solution.py:52
  273.5 10.5 %collective-permute-done.29 = bf16[64,3328]{1,0:T(8,128)(2,1)S(1)} collective-permute-done((bf16[64,3328]{1,0:T(8,128)(2,1)S(1)}, bf16[64,3328]{1,0:T(8,128)(2,1)S(1)}, u32[]{:S(2)}, u32[]{:S(2)}) %collective-permute-start.29) | collective-permute-done | bytes 426016 | tf_op jit(solution)/shard_map/ppermute | solution.py:52
  289.9 9.4 %collective-permute-done.6 = bf16[64,3328]{1,0:T(8,128)(2,1)S(1)} collective-permute-done((bf16[64,3328]{1,0:T(8,128)(2,1)S(1)}, bf16[64,3328]{1,0:T(8,128)(2,1)S(1)}, u32[]{:S(2)}, u32[]{:S(2)}) %collective-permute-start.6) | collective-permute-done | bytes 426016 | tf_op jit(solution)/shard_map/ppermute | solution.py:52
  301.0 9.4 %collective-permute-done.52 = bf16[64,3328]{1,0:T(8,128)(2,1)S(1)} collective-permute-done((bf16[64,3328]{1,0:T(8,128)(2,1)S(1)}, bf16[64,3328]{1,0:T(8,128)(2,1)S(1)}, u32[]{:S(2)}, u32[]{:S(2)}) %collective-permute-start.52) | collective-permute-done | bytes 426016 | tf_op jit(solution)/shard_map/ppermute | solution.py:52
  315.3 10.6 %collective-permute-done.76 = bf16[64,3328]{1,0:T(8,128)(2,1)S(1)} collective-permute-done((bf16[64,3328]{1,0:T(8,128)(2,1)S(1)}, bf16[64,3328]{1,0:T(8,128)(2,1)S(1)}, u32[]{:S(2)}, u32[]{:S(2)}) %collective-permute-start.76) | collective-permute-done | bytes 426016 | tf_op jit(solution)/shard_map/ppermute | solution.py:52
  326.3 10.5 %collective-permute-done.30 = bf16[64,3328]{1,0:T(8,128)(2,1)S(1)} collective-permute-done((bf16[64,3328]{1,0:T(8,128)(2,1)S(1)}, bf16[64,3328]{1,0:T(8,128)(2,1)S(1)}, u32[]{:S(2)}, u32[]{:S(2)}) %collective-permute-start.30) | collective-permute-done | bytes 426016 | tf_op jit(solution)/shard_map/ppermute | solution.py:52
  342.8 9.4 %collective-permute-done.7 = bf16[64,3328]{1,0:T(8,128)(2,1)S(1)} collective-permute-done((bf16[64,3328]{1,0:T(8,128)(2,1)S(1)}, bf16[64,3328]{1,0:T(8,128)(2,1)S(1)}, u32[]{:S(2)}, u32[]{:S(2)}) %collective-permute-start.7) | collective-permute-done | bytes 426016 | tf_op jit(solution)/shard_map/ppermute | solution.py:52
  353.9 9.4 %collective-permute-done.53 = bf16[64,3328]{1,0:T(8,128)(2,1)S(1)} collective-permute-done((bf16[64,3328]{1,0:T(8,128)(2,1)S(1)}, bf16[64,3328]{1,0:T(8,128)(2,1)S(1)}, u32[]{:S(2)}, u32[]{:S(2)}) %collective-permute-start.53) | collective-permute-done | bytes 426016 | tf_op jit(solution)/shard_map/ppermute | solution.py:52
  368.1 10.6 %collective-permute-done.77 = bf16[64,3328]{1,0:T(8,128)(2,1)S(1)} collective-permute-done((bf16[64,3328]{1,0:T(8,128)(2,1)S(1)}, bf16[64,3328]{1,0:T(8,128)(2,1)S(1)}, u32[]{:S(2)}, u32[]{:S(2)}) %collective-permute-start.77) | collective-permute-done | bytes 426016 | tf_op jit(solution)/shard_map/ppermute | solution.py:52
  379.2 10.5 %collective-permute-done.31 = bf16[64,3328]{1,0:T(8,128)(2,1)S(1)} collective-permute-done((bf16[64,3328]{1,0:T(8,128)(2,1)S(1)}, bf16[64,3328]{1,0:T(8,128)(2,1)S(1)}, u32[]{:S(2)}, u32[]{:S(2)}) %collective-permute-start.31) | collective-permute-done | bytes 426016 | tf_op jit(solution)/shard_map/ppermute | solution.py:52
  395.7 9.4 %collective-permute-done.8 = bf16[64,3328]{1,0:T(8,128)(2,1)S(1)} collective-permute-done((bf16[64,3328]{1,0:T(8,128)(2,1)S(1)}, bf16[64,3328]{1,0:T(8,128)(2,1)S(1)}, u32[]{:S(2)}, u32[]{:S(2)}) %collective-permute-start.8) | collective-permute-done | bytes 426016 | tf_op jit(solution)/shard_map/ppermute | solution.py:52
  406.8 9.4 %collective-permute-done.54 = bf16[64,3328]{1,0:T(8,128)(2,1)S(1)} collective-permute-done((bf16[64,3328]{1,0:T(8,128)(2,1)S(1)}, bf16[64,3328]{1,0:T(8,128)(2,1)S(1)}, u32[]{:S(2)}, u32[]{:S(2)}) %collective-permute-start.54) | collective-permute-done | bytes 426016 | tf_op jit(solution)/shard_map/ppermute | solution.py:52
  424.0 2.1 fusion.72
  427.8 2.1 fusion.73
  433.9 8.7 %collective-permute-done.32 = bf16[64,3328]{1,0:T(8,128)(2,1)S(1)} collective-permute-done((bf16[64,3328]{1,0:T(8,128)(2,1)S(1)}, bf16[64,3328]{1,0:T(8,128)(2,1)S(1)}, u32[]{:S(2)}, u32[]{:S(2)}) %collective-permute-start.32) | collective-permute-done | bytes 426016 | tf_op jit(solution)/shard_map/ppermute | solution.py:52
  442.6 2.6 fusion.63
  453.8 2.5 fusion.71
  457.9 10.5 %convolution_multiply_fusion = f32[3328,1024]{1,0:T(8,128)} fusion(bf16[1024,3328]{1,0:T(8,128)(2,1)S(1)} %bitcast.316, bf16[1024,1024]{1,0:T(8,128)(2,1)S(1)} %bitcast.309), kind=kOutput, calls=%fused_computation.3 | convolution fusion | flops 6982729728 | bytes 22544384 | tf_op jit(solution)/shard_map/dot_general | solution.py:118
  468.4 21.2 %dynamic_update_slice.276 = f32[13312,1024]{1,0:T(8,128)} pad(f32[3328,1024]{1,0:T(8,128)} %convolution_multiply_fusion, f32[]{:T(128)} %constant.33.clone.1), padding=0_9984x0_0 | pad | bytes 68157440 | tf_op jit(solution)/shard_map/dynamic_update_slice | solution.py:121
  489.6 2.0 fusion.54
  493.2 2.0 fusion.46
  495.7 3.1 fusion.62
  499.2 2.8 fusion.70
  503.6 13.5 %multiply_dynamic-update-slice_fusion.2 = f32[13312,1024]{1,0:T(8,128)} fusion(f32[13312,1024]{1,0:T(8,128)} %dynamic_update_slice.276, bf16[1024,3328]{1,0:T(8,128)(2,1)} %bitcast.127, bf16[1024,1024]{1,0:T(8,128)(2,1)S(1)} %bitcast.310), kind=kOutput, calls=%fused_computation.2 | convolution fusion | flops 6982729728 | bytes 22544384 | tf_op jit(solution)/shard_map/dot_general | solution.py:118
  519.4 1.9 fusion.61
  521.9 2.7 fusion.69
  527.9 1.9 collective-permute-start.66
  529.8 10.5 %multiply_dynamic-update-slice_fusion.1 = f32[13312,1024]{1,0:T(8,128)} fusion(f32[13312,1024]{1,0:T(8,128)} %multiply_dynamic-update-slice_fusion.2, bf16[1024,3328]{1,0:T(8,128)(2,1)S(1)} %bitcast.319, bf16[1024,1024]{1,0:T(8,128)(2,1)S(1)} %bitcast.311), kind=kOutput, calls=%fused_computation.1 | convolution fusion | flops 6982729728 | bytes 22544384 | tf_op jit(solution)/shard_map/dot_general | solution.py:118
  542.5 1.9 fusion.60
  544.9 1.9 fusion.68
  551.8 3.1 collective-permute-done.90
  554.9 1.9 fusion.43
  557.2 6.8 %collective-permute-done.44 = bf16[64,3328]{1,0:T(8,128)(2,1)S(1)} collective-permute-done((bf16[64,3328]{1,0:T(8,128)(2,1)S(1)}, bf16[64,3328]{1,0:T(8,128)(2,1)S(1)}, u32[]{:S(2)}, u32[]{:S(2)}) %collective-permute-start.44) | collective-permute-done | bytes 426016 | tf_op jit(solution)/shard_map/ppermute | solution.py:52
  564.0 1.9 fusion.59
  575.5 6.7 %collective-permute-done.45 = bf16[64,3328]{1,0:T(8,128)(2,1)S(1)} collective-permute-done((bf16[64,3328]{1,0:T(8,128)(2,1)S(1)}, bf16[64,3328]{1,0:T(8,128)(2,1)S(1)}, u32[]{:S(2)}, u32[]{:S(2)}) %collective-permute-start.45) | collective-permute-done | bytes 426016 | tf_op jit(solution)/shard_map/ppermute | solution.py:52
  591.3 10.5 %multiply_dynamic-update-slice_fusion = f32[13312,1024]{1,0:T(8,128)} fusion(f32[13312,1024]{1,0:T(8,128)} %multiply_dynamic-update-slice_fusion.1, bf16[1024,3328]{1,0:T(8,128)(2,1)S(1)} %bitcast.315, bf16[1024,1024]{1,0:T(8,128)(2,1)S(1)} %bitcast.312), kind=kOutput, calls=%fused_computation | convolution fusion | flops 6982729728 | bytes 22544384 | tf_op jit(solution)/shard_map/dot_general | solution.py:118
  601.8 3.7 fusion.65
  (282 shorter events, 156.1 us)
Async XLA Ops:
  3.4 52.5 %collective-permute-start.10 = (bf16[64,3328]{1,0:T(8,128)(2,1)}, bf16[64,3328]{1,0:T(8,128)(2,1)}, u32[]{:S(2)}, u32[]{:S(2)}) collective-permute-start(bf16[64,3328]{1,0:T(8,128)(2,1)} %get-tuple-element.32), channel_id=1, source_target_pairs={{0,2},{2,0},{4,6},{6,4},{8,10},{10,8},{12,14},{14,12},{16,18},{18,... | collective-permute-start | bytes 1277960 | tf_op jit(solution)/shard_map/ppermute | solution.py:55
  3.8 49.4 %collective-permute-start.2 = (bf16[64,3328]{1,0:T(8,128)(2,1)}, bf16[64,3328]{1,0:T(8,128)(2,1)}, u32[]{:S(2)}, u32[]{:S(2)}) collective-permute-start(bf16[64,3328]{1,0:T(8,128)(2,1)} %get-tuple-element.32), channel_id=1, source_target_pairs={{0,8},{2,10},{8,16},{10,18},{16,24},{18,26},{24,28},{26,30},{28,20... | collective-permute-start | bytes 1277960 | tf_op jit(solution)/shard_map/ppermute | solution.py:52
  6.4 98.7 %collective-permute-start = (bf16[512,1024]{1,0:T(8,128)(2,1)}, bf16[512,1024]{1,0:T(8,128)(2,1)}, u32[]{:S(2)}, u32[]{:S(2)}) collective-permute-start(bf16[512,1024]{1,0:T(8,128)(2,1)} %param.5), channel_id=1, source_target_pairs={{0,1},{1,0},{2,3},{3,2},{4,5},{5,4},{6,7},{7,6},{8,9},{9,8},{10,11... | collective-permute-start | bytes 3145736 | tf_op jit(solution)/shard_map/ppermute | solution.py:66
  7.9 26.2 %collective-permute-start.34 = (bf16[64,3328]{1,0:T(8,128)(2,1)}, bf16[64,3328]{1,0:T(8,128)(2,1)}, u32[]{:S(2)}, u32[]{:S(2)}) collective-permute-start(bf16[64,3328]{1,0:T(8,128)(2,1)} %get-tuple-element.33), channel_id=1, source_target_pairs={{0,2},{2,0},{4,6},{6,4},{8,10},{10,8},{12,14},{14,12},{16,18},{18,... | collective-permute-start | bytes 1277960 | tf_op jit(solution)/shard_map/ppermute | solution.py:55
  7.9 23.4 %collective-permute-start.82 = (bf16[64,3328]{1,0:T(8,128)(2,1)}, bf16[64,3328]{1,0:T(8,128)(2,1)}, u32[]{:S(2)}, u32[]{:S(2)}) collective-permute-start(bf16[64,3328]{1,0:T(8,128)(2,1)} %get-tuple-element.34), channel_id=1, source_target_pairs={{0,2},{2,0},{4,6},{6,4},{8,10},{10,8},{12,14},{14,12},{16,18},{18,... | collective-permute-start | bytes 1277960 | tf_op jit(solution)/shard_map/ppermute | solution.py:55
  31.3 23.5 %collective-permute-start.25 = (bf16[64,3328]{1,0:T(8,128)(2,1)}, bf16[64,3328]{1,0:T(8,128)(2,1)S(1)}, u32[]{:S(2)}, u32[]{:S(2)}) collective-permute-start(bf16[64,3328]{1,0:T(8,128)(2,1)} %get-tuple-element.33), channel_id=1, source_target_pairs={{0,4},{2,6},{8,0},{10,2},{16,8},{18,10},{24,16},{26,18},{28,24},{3... | collective-permute-start | bytes 1277960 | tf_op jit(solution)/shard_map/ppermute | solution.py:52
  34.1 18.3 %collective-permute-start.71 = (bf16[64,3328]{1,0:T(8,128)(2,1)}, bf16[64,3328]{1,0:T(8,128)(2,1)S(1)}, u32[]{:S(2)}, u32[]{:S(2)}) collective-permute-start(bf16[64,3328]{1,0:T(8,128)(2,1)} %get-tuple-element.34), channel_id=1, source_target_pairs={{0,4},{2,6},{8,0},{10,2},{16,8},{18,10},{24,16},{26,18},{28,24},{3... | collective-permute-start | bytes 1277960 | tf_op jit(solution)/shard_map/ppermute | solution.py:52
  53.2 12.8 %collective-permute-start.48 = (bf16[64,3328]{1,0:T(8,128)(2,1)}, bf16[64,3328]{1,0:T(8,128)(2,1)S(1)}, u32[]{:S(2)}, u32[]{:S(2)}) collective-permute-start(bf16[64,3328]{1,0:T(8,128)(2,1)} %get-tuple-element.35), channel_id=1, source_target_pairs={{0,8},{2,10},{8,16},{10,18},{16,24},{18,26},{24,28},{26,30},{28,20... | collective-permute-start | bytes 1277960 | tf_op jit(solution)/shard_map/ppermute | solution.py:52
  54.9 39.6 %collective-permute-start.11 = (bf16[64,3328]{1,0:T(8,128)(2,1)}, bf16[64,3328]{1,0:T(8,128)(2,1)S(1)}, u32[]{:S(2)}, u32[]{:S(2)}) collective-permute-start(bf16[64,3328]{1,0:T(8,128)(2,1)} %collective-permute-done.2), channel_id=1, source_target_pairs={{0,2},{2,0},{4,6},{6,4},{8,10},{10,8},{12,14},{14,12},{16,18},{18,... | collective-permute-start | bytes 1277960 | tf_op jit(solution)/shard_map/ppermute | solution.py:55
  55.9 34.9 %collective-permute-start.3 = (bf16[64,3328]{1,0:T(8,128)(2,1)}, bf16[64,3328]{1,0:T(8,128)(2,1)S(1)}, u32[]{:S(2)}, u32[]{:S(2)}) collective-permute-start(bf16[64,3328]{1,0:T(8,128)(2,1)} %collective-permute-done.2), channel_id=1, source_target_pairs={{0,8},{2,10},{8,16},{10,18},{16,24},{18,26},{24,28},{26,30},{28,20... | collective-permute-start | bytes 1277960 | tf_op jit(solution)/shard_map/ppermute | solution.py:52
  67.8 24.5 %collective-permute-start.26 = (bf16[64,3328]{1,0:T(8,128)(2,1)S(1)}, bf16[64,3328]{1,0:T(8,128)(2,1)}, u32[]{:S(2)}, u32[]{:S(2)}) collective-permute-start(bf16[64,3328]{1,0:T(8,128)(2,1)S(1)} %collective-permute-done.25), channel_id=1, source_target_pairs={{0,4},{2,6},{8,0},{10,2},{16,8},{18,10},{24,16},{26,18},{28,24},{3... | collective-permute-start | bytes 1277960 | tf_op jit(solution)/shard_map/ppermute | solution.py:52
  69.1 19.8 %collective-permute-start.72 = (bf16[64,3328]{1,0:T(8,128)(2,1)S(1)}, bf16[64,3328]{1,0:T(8,128)(2,1)}, u32[]{:S(2)}, u32[]{:S(2)}) collective-permute-start(bf16[64,3328]{1,0:T(8,128)(2,1)S(1)} %collective-permute-done.71), channel_id=1, source_target_pairs={{0,4},{2,6},{8,0},{10,2},{16,8},{18,10},{24,16},{26,18},{28,24},{3... | collective-permute-start | bytes 1277960 | tf_op jit(solution)/shard_map/ppermute | solution.py:52
  90.8 12.6 %collective-permute-start.49 = (bf16[64,3328]{1,0:T(8,128)(2,1)S(1)}, bf16[64,3328]{1,0:T(8,128)(2,1)S(1)}, u32[]{:S(2)}, u32[]{:S(2)}) collective-permute-start(bf16[64,3328]{1,0:T(8,128)(2,1)S(1)} %collective-permute-done.48), channel_id=1, source_target_pairs={{0,8},{2,10},{8,16},{10,18},{16,24},{18,26},{24,28},{26,30},{28,20... | collective-permute-start | bytes 1277960 | tf_op jit(solution)/shard_map/ppermute | solution.py:52
  92.4 95.4 %collective-permute-start.12 = (bf16[64,3328]{1,0:T(8,128)(2,1)S(1)}, bf16[64,3328]{1,0:T(8,128)(2,1)}, u32[]{:S(2)}, u32[]{:S(2)}) collective-permute-start(bf16[64,3328]{1,0:T(8,128)(2,1)S(1)} %collective-permute-done.3), channel_id=1, source_target_pairs={{0,2},{2,0},{4,6},{6,4},{8,10},{10,8},{12,14},{14,12},{16,18},{18,... | collective-permute-start | bytes 1277960 | tf_op jit(solution)/shard_map/ppermute | solution.py:55
  94.4 95.8 %collective-permute-start.4 = (bf16[64,3328]{1,0:T(8,128)(2,1)S(1)}, bf16[64,3328]{1,0:T(8,128)(2,1)S(1)}, u32[]{:S(2)}, u32[]{:S(2)}) collective-permute-start(bf16[64,3328]{1,0:T(8,128)(2,1)S(1)} %collective-permute-done.3), channel_id=1, source_target_pairs={{0,8},{2,10},{8,16},{10,18},{16,24},{18,26},{24,28},{26,30},{28,20... | collective-permute-start | bytes 1277960 | tf_op jit(solution)/shard_map/ppermute | solution.py:52
  96.0 78.3 %collective-permute-start.36 = (bf16[64,3328]{1,0:T(8,128)(2,1)}, bf16[64,3328]{1,0:T(8,128)(2,1)}, u32[]{:S(2)}, u32[]{:S(2)}) collective-permute-start(bf16[64,3328]{1,0:T(8,128)(2,1)} %collective-permute-done.26), channel_id=1, source_target_pairs={{0,2},{2,0},{4,6},{6,4},{8,10},{10,8},{12,14},{14,12},{16,18},{18,... | collective-permute-start | bytes 1277960 | tf_op jit(solution)/shard_map/ppermute | solution.py:55
  103.4 82.5 %collective-permute-start.27 = (bf16[64,3328]{1,0:T(8,128)(2,1)}, bf16[64,3328]{1,0:T(8,128)(2,1)}, u32[]{:S(2)}, u32[]{:S(2)}) collective-permute-start(bf16[64,3328]{1,0:T(8,128)(2,1)} %collective-permute-done.26), channel_id=1, source_target_pairs={{0,4},{2,6},{8,0},{10,2},{16,8},{18,10},{24,16},{26,18},{28,24},{3... | collective-permute-start | bytes 1277960 | tf_op jit(solution)/shard_map/ppermute | solution.py:52
  105.1 66.7 %collective-permute-start.84 = (bf16[64,3328]{1,0:T(8,128)(2,1)}, bf16[64,3328]{1,0:T(8,128)(2,1)}, u32[]{:S(2)}, u32[]{:S(2)}) collective-permute-start(bf16[64,3328]{1,0:T(8,128)(2,1)} %collective-permute-done.72), channel_id=1, source_target_pairs={{0,2},{2,0},{4,6},{6,4},{8,10},{10,8},{12,14},{14,12},{16,18},{18,... | collective-permute-start | bytes 1277960 | tf_op jit(solution)/shard_map/ppermute | solution.py:55
  171.8 12.4 %collective-permute-start.73 = (bf16[64,3328]{1,0:T(8,128)(2,1)}, bf16[64,3328]{1,0:T(8,128)(2,1)S(1)}, u32[]{:S(2)}, u32[]{:S(2)}) collective-permute-start(bf16[64,3328]{1,0:T(8,128)(2,1)} %collective-permute-done.72), channel_id=1, source_target_pairs={{0,4},{2,6},{8,0},{10,2},{16,8},{18,10},{24,16},{26,18},{28,24},{3... | collective-permute-start | bytes 1277960 | tf_op jit(solution)/shard_map/ppermute | solution.py:52
  174.4 14.9 %collective-permute-start.60 = (bf16[64,3328]{1,0:T(8,128)(2,1)S(1)}, bf16[64,3328]{1,0:T(8,128)(2,1)S(1)}, u32[]{:S(2)}, u32[]{:S(2)}) collective-permute-start(bf16[64,3328]{1,0:T(8,128)(2,1)S(1)} %collective-permute-done.49), channel_id=1, source_target_pairs={{0,2},{2,0},{4,6},{6,4},{8,10},{10,8},{12,14},{14,12},{16,18},{18,... | collective-permute-start | bytes 1277960 | tf_op jit(solution)/shard_map/ppermute | solution.py:55
  184.3 11.4 %collective-permute-start.50 = (bf16[64,3328]{1,0:T(8,128)(2,1)S(1)}, bf16[64,3328]{1,0:T(8,128)(2,1)S(1)}, u32[]{:S(2)}, u32[]{:S(2)}) collective-permute-start(bf16[64,3328]{1,0:T(8,128)(2,1)S(1)} %collective-permute-done.49), channel_id=1, source_target_pairs={{0,8},{2,10},{8,16},{10,18},{16,24},{18,26},{24,28},{26,30},{28,20... | collective-permute-start | bytes 1277960 | tf_op jit(solution)/shard_map/ppermute | solution.py:52
  185.9 238.2 %collective-permute-start.1 = (bf16[8,64,3328]{2,1,0:T(8,128)(2,1)}, bf16[8,64,3328]{2,1,0:T(8,128)(2,1)S(1)}, u32[]{:S(2)}, u32[]{:S(2)}) collective-permute-start(bf16[8,64,3328]{2,1,0:T(8,128)(2,1)} %bitcast.363), channel_id=1, source_target_pairs={{0,2},{2,0},{4,6},{6,4},{8,10},{10,8},{12,14},{14,12},{16,18},{18,... | collective-permute-start | bytes 10223624 | tf_op jit(solution)/shard_map/ppermute | solution.py:55
  187.8 240.0 %collective-permute-start.24 = (bf16[8,64,3328]{2,1,0:T(8,128)(2,1)}, bf16[8,64,3328]{2,1,0:T(8,128)(2,1)S(1)}, u32[]{:S(2)}, u32[]{:S(2)}) collective-permute-start(bf16[8,64,3328]{2,1,0:T(8,128)(2,1)} %bitcast.362), channel_id=1, source_target_pairs={{0,2},{2,0},{4,6},{6,4},{8,10},{10,8},{12,14},{14,12},{16,18},{18,... | collective-permute-start | bytes 10223624 | tf_op jit(solution)/shard_map/ppermute | solution.py:55
  189.3 241.0 %collective-permute-start.47 = (bf16[8,64,3328]{2,1,0:T(8,128)(2,1)}, bf16[8,64,3328]{2,1,0:T(8,128)(2,1)S(1)}, u32[]{:S(2)}, u32[]{:S(2)}) collective-permute-start(bf16[8,64,3328]{2,1,0:T(8,128)(2,1)} %bitcast.361), channel_id=1, source_target_pairs={{0,2},{2,0},{4,6},{6,4},{8,10},{10,8},{12,14},{14,12},{16,18},{18,... | collective-permute-start | bytes 10223624 | tf_op jit(solution)/shard_map/ppermute | solution.py:55
  190.2 242.6 %collective-permute-start.70 = (bf16[8,64,3328]{2,1,0:T(8,128)(2,1)}, bf16[8,64,3328]{2,1,0:T(8,128)(2,1)S(1)}, u32[]{:S(2)}, u32[]{:S(2)}) collective-permute-start(bf16[8,64,3328]{2,1,0:T(8,128)(2,1)} %bitcast.360), channel_id=1, source_target_pairs={{0,2},{2,0},{4,6},{6,4},{8,10},{10,8},{12,14},{14,12},{16,18},{18,... | collective-permute-start | bytes 10223624 | tf_op jit(solution)/shard_map/ppermute | solution.py:55
  208.0 11.9 %collective-permute-start.74 = (bf16[64,3328]{1,0:T(8,128)(2,1)S(1)}, bf16[64,3328]{1,0:T(8,128)(2,1)S(1)}, u32[]{:S(2)}, u32[]{:S(2)}) collective-permute-start(bf16[64,3328]{1,0:T(8,128)(2,1)S(1)} %collective-permute-done.73), channel_id=1, source_target_pairs={{0,4},{2,6},{8,0},{10,2},{16,8},{18,10},{24,16},{26,18},{28,24},{3... | collective-permute-start | bytes 1277960 | tf_op jit(solution)/shard_map/ppermute | solution.py:52
  219.9 11.2 %collective-permute-start.28 = (bf16[64,3328]{1,0:T(8,128)(2,1)}, bf16[64,3328]{1,0:T(8,128)(2,1)S(1)}, u32[]{:S(2)}, u32[]{:S(2)}) collective-permute-start(bf16[64,3328]{1,0:T(8,128)(2,1)} %collective-permute-done.27), channel_id=1, source_target_pairs={{0,4},{2,6},{8,0},{10,2},{16,8},{18,10},{24,16},{26,18},{28,24},{3... | collective-permute-start | bytes 1277960 | tf_op jit(solution)/shard_map/ppermute | solution.py:52
  234.7 11.9 %collective-permute-start.5 = (bf16[64,3328]{1,0:T(8,128)(2,1)S(1)}, bf16[64,3328]{1,0:T(8,128)(2,1)S(1)}, u32[]{:S(2)}, u32[]{:S(2)}) collective-permute-start(bf16[64,3328]{1,0:T(8,128)(2,1)S(1)} %collective-permute-done.4), channel_id=1, source_target_pairs={{0,8},{2,10},{8,16},{10,18},{16,24},{18,26},{24,28},{26,30},{28,20... | collective-permute-start | bytes 1277960 | tf_op jit(solution)/shard_map/ppermute | solution.py:52
  261.1 11.9 %collective-permute-start.75 = (bf16[64,3328]{1,0:T(8,128)(2,1)S(1)}, bf16[64,3328]{1,0:T(8,128)(2,1)S(1)}, u32[]{:S(2)}, u32[]{:S(2)}) collective-permute-start(bf16[64,3328]{1,0:T(8,128)(2,1)S(1)} %collective-permute-done.74), channel_id=1, source_target_pairs={{0,4},{2,6},{8,0},{10,2},{16,8},{18,10},{24,16},{26,18},{28,24},{3... | collective-permute-start | bytes 1277960 | tf_op jit(solution)/shard_map/ppermute | solution.py:52
  273.0 11.0 %collective-permute-start.29 = (bf16[64,3328]{1,0:T(8,128)(2,1)S(1)}, bf16[64,3328]{1,0:T(8,128)(2,1)S(1)}, u32[]{:S(2)}, u32[]{:S(2)}) collective-permute-start(bf16[64,3328]{1,0:T(8,128)(2,1)S(1)} %collective-permute-done.28), channel_id=1, source_target_pairs={{0,4},{2,6},{8,0},{10,2},{16,8},{18,10},{24,16},{26,18},{28,24},{3... | collective-permute-start | bytes 1277960 | tf_op jit(solution)/shard_map/ppermute | solution.py:52
  287.5 11.9 %collective-permute-start.6 = (bf16[64,3328]{1,0:T(8,128)(2,1)S(1)}, bf16[64,3328]{1,0:T(8,128)(2,1)S(1)}, u32[]{:S(2)}, u32[]{:S(2)}) collective-permute-start(bf16[64,3328]{1,0:T(8,128)(2,1)S(1)} %collective-permute-done.5), channel_id=1, source_target_pairs={{0,8},{2,10},{8,16},{10,18},{16,24},{18,26},{24,28},{26,30},{28,20... | collective-permute-start | bytes 1277960 | tf_op jit(solution)/shard_map/ppermute | solution.py:52
  299.4 11.0 %collective-permute-start.52 = (bf16[64,3328]{1,0:T(8,128)(2,1)S(1)}, bf16[64,3328]{1,0:T(8,128)(2,1)S(1)}, u32[]{:S(2)}, u32[]{:S(2)}) collective-permute-start(bf16[64,3328]{1,0:T(8,128)(2,1)S(1)} %collective-permute-done.51), channel_id=1, source_target_pairs={{0,8},{2,10},{8,16},{10,18},{16,24},{18,26},{24,28},{26,30},{28,20... | collective-permute-start | bytes 1277960 | tf_op jit(solution)/shard_map/ppermute | solution.py:52
  314.0 11.9 %collective-permute-start.76 = (bf16[64,3328]{1,0:T(8,128)(2,1)S(1)}, bf16[64,3328]{1,0:T(8,128)(2,1)S(1)}, u32[]{:S(2)}, u32[]{:S(2)}) collective-permute-start(bf16[64,3328]{1,0:T(8,128)(2,1)S(1)} %collective-permute-done.75), channel_id=1, source_target_pairs={{0,4},{2,6},{8,0},{10,2},{16,8},{18,10},{24,16},{26,18},{28,24},{3... | collective-permute-start | bytes 1277960 | tf_op jit(solution)/shard_map/ppermute | solution.py:52
  340.4 11.9 %collective-permute-start.7 = (bf16[64,3328]{1,0:T(8,128)(2,1)S(1)}, bf16[64,3328]{1,0:T(8,128)(2,1)S(1)}, u32[]{:S(2)}, u32[]{:S(2)}) collective-permute-start(bf16[64,3328]{1,0:T(8,128)(2,1)S(1)} %collective-permute-done.6), channel_id=1, source_target_pairs={{0,8},{2,10},{8,16},{10,18},{16,24},{18,26},{24,28},{26,30},{28,20... | collective-permute-start | bytes 1277960 | tf_op jit(solution)/shard_map/ppermute | solution.py:52
  366.8 11.9 %collective-permute-start.77 = (bf16[64,3328]{1,0:T(8,128)(2,1)S(1)}, bf16[64,3328]{1,0:T(8,128)(2,1)S(1)}, u32[]{:S(2)}, u32[]{:S(2)}) collective-permute-start(bf16[64,3328]{1,0:T(8,128)(2,1)S(1)} %collective-permute-done.76), channel_id=1, source_target_pairs={{0,4},{2,6},{8,0},{10,2},{16,8},{18,10},{24,16},{26,18},{28,24},{3... | collective-permute-start | bytes 1277960 | tf_op jit(solution)/shard_map/ppermute | solution.py:52
  393.3 11.9 %collective-permute-start.8 = (bf16[64,3328]{1,0:T(8,128)(2,1)S(1)}, bf16[64,3328]{1,0:T(8,128)(2,1)S(1)}, u32[]{:S(2)}, u32[]{:S(2)}) collective-permute-start(bf16[64,3328]{1,0:T(8,128)(2,1)S(1)} %collective-permute-done.7), channel_id=1, source_target_pairs={{0,8},{2,10},{8,16},{10,18},{16,24},{18,26},{24,28},{26,30},{28,20... | collective-permute-start | bytes 1277960 | tf_op jit(solution)/shard_map/ppermute | solution.py:52
  426.1 27.7 %collective-permute-start.9 = (bf16[64,3328]{1,0:T(8,128)(2,1)S(1)}, bf16[64,3328]{1,0:T(8,128)(2,1)S(1)}, u32[]{:S(2)}, u32[]{:S(2)}) collective-permute-start(bf16[64,3328]{1,0:T(8,128)(2,1)S(1)} %fusion.72), channel_id=1, source_target_pairs={{0,8},{2,10},{8,16},{10,18},{16,24},{18,26},{24,28},{26,30},{28,20... | collective-permute-start | bytes 1277960 | tf_op jit(solution)/shard_map/ppermute | solution.py:52
  429.9 12.8 %collective-permute-start.32 = (bf16[64,3328]{1,0:T(8,128)(2,1)S(1)}, bf16[64,3328]{1,0:T(8,128)(2,1)S(1)}, u32[]{:S(2)}, u32[]{:S(2)}) collective-permute-start(bf16[64,3328]{1,0:T(8,128)(2,1)S(1)} %fusion.73), channel_id=1, source_target_pairs={{0,4},{2,6},{8,0},{10,2},{16,8},{18,10},{24,16},{26,18},{28,24},{3... | collective-permute-start | bytes 1277960 | tf_op jit(solution)/shard_map/ppermute | solution.py:52
  431.0 16.1 %collective-permute-start.55 = (bf16[64,3328]{1,0:T(8,128)(2,1)S(1)}, bf16[64,3328]{1,0:T(8,128)(2,1)S(1)}, u32[]{:S(2)}, u32[]{:S(2)}) collective-permute-start(bf16[64,3328]{1,0:T(8,128)(2,1)S(1)} %fusion.74), channel_id=1, source_target_pairs={{0,8},{2,10},{8,16},{10,18},{16,24},{18,26},{24,28},{26,30},{28,20... | collective-permute-start | bytes 1277960 | tf_op jit(solution)/shard_map/ppermute | solution.py:52
  433.5 18.3 %collective-permute-start.78 = (bf16[64,3328]{1,0:T(8,128)(2,1)S(1)}, bf16[64,3328]{1,0:T(8,128)(2,1)S(1)}, u32[]{:S(2)}, u32[]{:S(2)}) collective-permute-start(bf16[64,3328]{1,0:T(8,128)(2,1)S(1)} %fusion.75), channel_id=1, source_target_pairs={{0,4},{2,6},{8,0},{10,2},{16,8},{18,10},{24,16},{26,18},{28,24},{3... | collective-permute-start | bytes 1277960 | tf_op jit(solution)/shard_map/ppermute | solution.py:52
  445.2 50.5 %collective-permute-start.33 = (bf16[64,3328]{1,0:T(8,128)(2,1)}, bf16[64,3328]{1,0:T(8,128)(2,1)S(1)}, u32[]{:S(2)}, u32[]{:S(2)}) collective-permute-start(bf16[64,3328]{1,0:T(8,128)(2,1)} %fusion.63), channel_id=1, source_target_pairs={{0,4},{2,6},{8,0},{10,2},{16,8},{18,10},{24,16},{26,18},{28,24},{3... | collective-permute-start | bytes 1277960 | tf_op jit(solution)/shard_map/ppermute | solution.py:52
  448.7 40.9 %collective-permute-start.56 = (bf16[64,3328]{1,0:T(8,128)(2,1)}, bf16[64,3328]{1,0:T(8,128)(2,1)}, u32[]{:S(2)}, u32[]{:S(2)}) collective-permute-start(bf16[64,3328]{1,0:T(8,128)(2,1)} %fusion.55), channel_id=1, source_target_pairs={{0,8},{2,10},{8,16},{10,18},{16,24},{18,26},{24,28},{26,30},{28,20... | collective-permute-start | bytes 1277960 | tf_op jit(solution)/shard_map/ppermute | solution.py:52
  453.4 39.8 %collective-permute-start.79 = (bf16[64,3328]{1,0:T(8,128)(2,1)}, bf16[64,3328]{1,0:T(8,128)(2,1)}, u32[]{:S(2)}, u32[]{:S(2)}) collective-permute-start(bf16[64,3328]{1,0:T(8,128)(2,1)} %fusion.47), channel_id=1, source_target_pairs={{0,4},{2,6},{8,0},{10,2},{16,8},{18,10},{24,16},{26,18},{28,24},{3... | collective-permute-start | bytes 1277960 | tf_op jit(solution)/shard_map/ppermute | solution.py:52
  456.3 42.9 %collective-permute-start.18 = (bf16[64,3328]{1,0:T(8,128)(2,1)}, bf16[64,3328]{1,0:T(8,128)(2,1)}, u32[]{:S(2)}, u32[]{:S(2)}) collective-permute-start(bf16[64,3328]{1,0:T(8,128)(2,1)} %fusion.71), channel_id=1, source_target_pairs={{0,8},{2,10},{8,16},{10,18},{16,24},{18,26},{24,28},{26,30},{28,20... | collective-permute-start | bytes 1277960 | tf_op jit(solution)/shard_map/ppermute | solution.py:52
  491.6 34.4 %collective-permute-start.57 = (bf16[64,3328]{1,0:T(8,128)(2,1)S(1)}, bf16[64,3328]{1,0:T(8,128)(2,1)S(1)}, u32[]{:S(2)}, u32[]{:S(2)}) collective-permute-start(bf16[64,3328]{1,0:T(8,128)(2,1)S(1)} %fusion.54), channel_id=1, source_target_pairs={{0,8},{2,10},{8,16},{10,18},{16,24},{18,26},{24,28},{26,30},{28,20... | collective-permute-start | bytes 1277960 | tf_op jit(solution)/shard_map/ppermute | solution.py:52
  495.1 22.0 %collective-permute-start.80 = (bf16[64,3328]{1,0:T(8,128)(2,1)S(1)}, bf16[64,3328]{1,0:T(8,128)(2,1)S(1)}, u32[]{:S(2)}, u32[]{:S(2)}) collective-permute-start(bf16[64,3328]{1,0:T(8,128)(2,1)S(1)} %fusion.46), channel_id=1, source_target_pairs={{0,4},{2,6},{8,0},{10,2},{16,8},{18,10},{24,16},{26,18},{28,24},{3... | collective-permute-start | bytes 1277960 | tf_op jit(solution)/shard_map/ppermute | solution.py:52
  498.8 20.5 %collective-permute-start.42 = (bf16[64,3328]{1,0:T(8,128)(2,1)}, bf16[64,3328]{1,0:T(8,128)(2,1)}, u32[]{:S(2)}, u32[]{:S(2)}) collective-permute-start(bf16[64,3328]{1,0:T(8,128)(2,1)} %fusion.62), channel_id=1, source_target_pairs={{0,4},{2,6},{8,0},{10,2},{16,8},{18,10},{24,16},{26,18},{28,24},{3... | collective-permute-start | bytes 1277960 | tf_op jit(solution)/shard_map/ppermute | solution.py:52
  502.0 19.9 %collective-permute-start.19 = (bf16[64,3328]{1,0:T(8,128)(2,1)}, bf16[64,3328]{1,0:T(8,128)(2,1)}, u32[]{:S(2)}, u32[]{:S(2)}) collective-permute-start(bf16[64,3328]{1,0:T(8,128)(2,1)} %fusion.70), channel_id=1, source_target_pairs={{0,8},{2,10},{8,16},{10,18},{16,24},{18,26},{24,28},{26,30},{28,20... | collective-permute-start | bytes 1277960 | tf_op jit(solution)/shard_map/ppermute | solution.py:52
  518.9 21.4 %collective-permute-start.81 = (bf16[64,3328]{1,0:T(8,128)(2,1)S(1)}, bf16[64,3328]{1,0:T(8,128)(2,1)S(1)}, u32[]{:S(2)}, u32[]{:S(2)}) collective-permute-start(bf16[64,3328]{1,0:T(8,128)(2,1)S(1)} %fusion.45), channel_id=1, source_target_pairs={{0,4},{2,6},{8,0},{10,2},{16,8},{18,10},{24,16},{26,18},{28,24},{3... | collective-permute-start | bytes 1277960 | tf_op jit(solution)/shard_map/ppermute | solution.py:52
  521.3 21.2 %collective-permute-start.43 = (bf16[64,3328]{1,0:T(8,128)(2,1)S(1)}, bf16[64,3328]{1,0:T(8,128)(2,1)}, u32[]{:S(2)}, u32[]{:S(2)}) collective-permute-start(bf16[64,3328]{1,0:T(8,128)(2,1)S(1)} %fusion.61), channel_id=1, source_target_pairs={{0,4},{2,6},{8,0},{10,2},{16,8},{18,10},{24,16},{26,18},{28,24},{3... | collective-permute-start | bytes 1277960 | tf_op jit(solution)/shard_map/ppermute | solution.py:52
  524.6 20.4 %collective-permute-start.20 = (bf16[64,3328]{1,0:T(8,128)(2,1)}, bf16[64,3328]{1,0:T(8,128)(2,1)}, u32[]{:S(2)}, u32[]{:S(2)}) collective-permute-start(bf16[64,3328]{1,0:T(8,128)(2,1)} %fusion.69), channel_id=1, source_target_pairs={{0,8},{2,10},{8,16},{10,18},{16,24},{18,26},{24,28},{26,30},{28,20... | collective-permute-start | bytes 1277960 | tf_op jit(solution)/shard_map/ppermute | solution.py:52
  527.9 20.5 %collective-permute-start.66 = (bf16[64,3328]{1,0:T(8,128)(2,1)S(1)}, bf16[64,3328]{1,0:T(8,128)(2,1)S(1)}, u32[]{:S(2)}, u32[]{:S(2)}) collective-permute-start(bf16[64,3328]{1,0:T(8,128)(2,1)S(1)} %fusion.53), channel_id=1, source_target_pairs={{0,8},{2,10},{8,16},{10,18},{16,24},{18,26},{24,28},{26,30},{28,20... | collective-permute-start | bytes 1277960 | tf_op jit(solution)/shard_map/ppermute | solution.py:52
  542.0 12.8 %collective-permute-start.90 = (bf16[64,3328]{1,0:T(8,128)(2,1)S(1)}, bf16[64,3328]{1,0:T(8,128)(2,1)S(1)}, u32[]{:S(2)}, u32[]{:S(2)}) collective-permute-start(bf16[64,3328]{1,0:T(8,128)(2,1)S(1)} %fusion.44), channel_id=1, source_target_pairs={{0,4},{2,6},{8,0},{10,2},{16,8},{18,10},{24,16},{26,18},{28,24},{3... | collective-permute-start | bytes 1277960 | tf_op jit(solution)/shard_map/ppermute | solution.py:52
  544.3 19.6 %collective-permute-start.44 = (bf16[64,3328]{1,0:T(8,128)(2,1)S(1)}, bf16[64,3328]{1,0:T(8,128)(2,1)S(1)}, u32[]{:S(2)}, u32[]{:S(2)}) collective-permute-start(bf16[64,3328]{1,0:T(8,128)(2,1)S(1)} %fusion.60), channel_id=1, source_target_pairs={{0,4},{2,6},{8,0},{10,2},{16,8},{18,10},{24,16},{26,18},{28,24},{3... | collective-permute-start | bytes 1277960 | tf_op jit(solution)/shard_map/ppermute | solution.py:52
  546.8 19.5 %collective-permute-start.21 = (bf16[64,3328]{1,0:T(8,128)(2,1)S(1)}, bf16[64,3328]{1,0:T(8,128)(2,1)S(1)}, u32[]{:S(2)}, u32[]{:S(2)}) collective-permute-start(bf16[64,3328]{1,0:T(8,128)(2,1)S(1)} %fusion.68), channel_id=1, source_target_pairs={{0,8},{2,10},{8,16},{10,18},{16,24},{18,26},{24,28},{26,30},{28,20... | collective-permute-start | bytes 1277960 | tf_op jit(solution)/shard_map/ppermute | solution.py:52
  550.1 19.7 %collective-permute-start.67 = (bf16[64,3328]{1,0:T(8,128)(2,1)S(1)}, bf16[64,3328]{1,0:T(8,128)(2,1)S(1)}, u32[]{:S(2)}, u32[]{:S(2)}) collective-permute-start(bf16[64,3328]{1,0:T(8,128)(2,1)S(1)} %fusion.52), channel_id=1, source_target_pairs={{0,8},{2,10},{8,16},{10,18},{16,24},{18,26},{24,28},{26,30},{28,20... | collective-permute-start | bytes 1277960 | tf_op jit(solution)/shard_map/ppermute | solution.py:52
  556.7 16.4 %collective-permute-start.91 = (bf16[64,3328]{1,0:T(8,128)(2,1)S(1)}, bf16[64,3328]{1,0:T(8,128)(2,1)S(1)}, u32[]{:S(2)}, u32[]{:S(2)}) collective-permute-start(bf16[64,3328]{1,0:T(8,128)(2,1)S(1)} %fusion.43), channel_id=1, source_target_pairs={{0,4},{2,6},{8,0},{10,2},{16,8},{18,10},{24,16},{26,18},{28,24},{3... | collective-permute-start | bytes 1277960 | tf_op jit(solution)/shard_map/ppermute | solution.py:52
  565.8 16.4 %collective-permute-start.45 = (bf16[64,3328]{1,0:T(8,128)(2,1)S(1)}, bf16[64,3328]{1,0:T(8,128)(2,1)S(1)}, u32[]{:S(2)}, u32[]{:S(2)}) collective-permute-start(bf16[64,3328]{1,0:T(8,128)(2,1)S(1)} %fusion.59), channel_id=1, source_target_pairs={{0,4},{2,6},{8,0},{10,2},{16,8},{18,10},{24,16},{26,18},{28,24},{3... | collective-permute-start | bytes 1277960 | tf_op jit(solution)/shard_map/ppermute | solution.py:52
  568.1 16.4 %collective-permute-start.22 = (bf16[64,3328]{1,0:T(8,128)(2,1)S(1)}, bf16[64,3328]{1,0:T(8,128)(2,1)S(1)}, u32[]{:S(2)}, u32[]{:S(2)}) collective-permute-start(bf16[64,3328]{1,0:T(8,128)(2,1)S(1)} %fusion.67), channel_id=1, source_target_pairs={{0,8},{2,10},{8,16},{10,18},{16,24},{18,26},{24,28},{26,30},{28,20... | collective-permute-start | bytes 1277960 | tf_op jit(solution)/shard_map/ppermute | solution.py:52
  571.6 16.4 %collective-permute-start.68 = (bf16[64,3328]{1,0:T(8,128)(2,1)S(1)}, bf16[64,3328]{1,0:T(8,128)(2,1)S(1)}, u32[]{:S(2)}, u32[]{:S(2)}) collective-permute-start(bf16[64,3328]{1,0:T(8,128)(2,1)S(1)} %fusion.51), channel_id=1, source_target_pairs={{0,8},{2,10},{8,16},{10,18},{16,24},{18,26},{24,28},{26,30},{28,20... | collective-permute-start | bytes 1277960 | tf_op jit(solution)/shard_map/ppermute | solution.py:52
  574.9 26.9 %collective-permute-start.92 = (bf16[64,3328]{1,0:T(8,128)(2,1)S(1)}, bf16[64,3328]{1,0:T(8,128)(2,1)S(1)}, u32[]{:S(2)}, u32[]{:S(2)}) collective-permute-start(bf16[64,3328]{1,0:T(8,128)(2,1)S(1)} %fusion.42), channel_id=1, source_target_pairs={{0,4},{2,6},{8,0},{10,2},{16,8},{18,10},{24,16},{26,18},{28,24},{3... | collective-permute-start | bytes 1277960 | tf_op jit(solution)/shard_map/ppermute | solution.py:52
  584.0 17.7 %collective-permute-start.46 = (bf16[64,3328]{1,0:T(8,128)(2,1)S(1)}, bf16[64,3328]{1,0:T(8,128)(2,1)S(1)}, u32[]{:S(2)}, u32[]{:S(2)}) collective-permute-start(bf16[64,3328]{1,0:T(8,128)(2,1)S(1)} %fusion.58), channel_id=1, source_target_pairs={{0,4},{2,6},{8,0},{10,2},{16,8},{18,10},{24,16},{26,18},{28,24},{3... | collective-permute-start | bytes 1277960 | tf_op jit(solution)/shard_map/ppermute | solution.py:52
  586.3 15.5 %collective-permute-start.23 = (bf16[64,3328]{1,0:T(8,128)(2,1)S(1)}, bf16[64,3328]{1,0:T(8,128)(2,1)S(1)}, u32[]{:S(2)}, u32[]{:S(2)}) collective-permute-start(bf16[64,3328]{1,0:T(8,128)(2,1)S(1)} %fusion.66), channel_id=1, source_target_pairs={{0,8},{2,10},{8,16},{10,18},{16,24},{18,26},{24,28},{26,30},{28,20... | collective-permute-start | bytes 1277960 | tf_op jit(solution)/shard_map/ppermute | solution.py:52
  589.8 12.0 %collective-permute-start.69 = (bf16[64,3328]{1,0:T(8,128)(2,1)S(1)}, bf16[64,3328]{1,0:T(8,128)(2,1)S(1)}, u32[]{:S(2)}, u32[]{:S(2)}) collective-permute-start(bf16[64,3328]{1,0:T(8,128)(2,1)S(1)} %fusion.50), channel_id=1, source_target_pairs={{0,8},{2,10},{8,16},{10,18},{16,24},{18,26},{24,28},{26,30},{28,20... | collective-permute-start | bytes 1277960 | tf_op jit(solution)/shard_map/ppermute | solution.py:52
  (49 other events, 796.6 us)

commit v2 on v1

--- a/solution.py
+++ b/solution.py
@@ -67,32 +67,45 @@
         grad_rows = put(grad_rows, other, lax.rem(tp_at - i + n_tp, n_tp))
     grad_rows = grad_rows.reshape(n_tp * part, -1)
 
+    split = grad_rows.reshape(chips, 2, rows, -1).transpose(1, 0, 2, 3)
+    ordered = jnp.stack([take(split, 1 - core), take(split, core)]).reshape(n * rows, -1)
+    nt = (((1,), (1,)), ((), ()))
+    tn = (((0,), (0,)), ((), ()))
+    scale = 1.0 / math.sqrt(n * rows)
+    weight_grad = jnp.zeros((width, ordered.shape[1]), jnp.float32)
+
     held = [hidden[:, c : c + piece] for c, _ in chains]
     own = list(held)
-    gathered = [jnp.zeros((n, rows, piece), hidden.dtype) for _ in chains]
-    for k, block in enumerate(held):
-        gathered[k] = put(gathered[k], block, me)
-        gathered[k] = put(gathered[k], swap(block), me + 1 - 2 * core)
+    gathered = [jnp.zeros((2, chips, rows, piece), hidden.dtype) for _ in chains]
+    my_chip = me // 2
+
+    def keep(into, block, chip):
+        return lax.dynamic_update_slice(
+            into, block[None, None], (1, chip, 0, 0), allow_negative_indices=False
+        )
+
+    gathered = [keep(g, block, my_chip) for g, block in zip(gathered, held)]
+    ours, theirs = [], []
+    count = len(chains)
     for s in range(1, chips):
         for k, (_, step) in enumerate(chains):
             held[k] = shift(held[k], step)
-            owner = chip_behind(step, s) * 2
-            gathered[k] = put(gathered[k], held[k], owner + core)
-            gathered[k] = put(gathered[k], swap(held[k]), owner + 1 - core)
-
-    split = grad_rows.reshape(chips, 2, rows, -1).transpose(1, 0, 2, 3)
-    nt = (((1,), (1,)), ((), ()))
-
-    def partial(c, k):
-        first = chains[k][0]
-        mine = take(split, c).reshape(chips * rows, -1)
-        out = lax.dot_general(
-            mine, weight[first : first + piece], nt, preferred_element_type=jnp.float32
-        )
-        return out.astype(jnp.bfloat16).reshape(chips, rows, piece)
-
-    theirs = [swap(partial(1 - core, k)) for k in range(len(chains))]
-    ours = [partial(core, k) for k in range(len(chains))]
+            gathered[k] = keep(gathered[k], held[k], chip_behind(step, s))
+        if s == 1:
+            held[0], weight_grad = lax.optimization_barrier((held[0], weight_grad))
+        k = s - 3
+        if 0 <= k < count:
+            held[k], theirs[k] = lax.optimization_barrier((held[k], theirs[k]))
+        k = s - 2
+        if 0 <= k < count:
+            held[k], rows_now = lax.optimization_barrier((held[k], ordered))
+            first = chains[k][0]
+            out = lax.dot_general(
+                rows_now, weight[first : first + piece], nt, preferred_element_type=jnp.float32
+            )
+            out = out.astype(jnp.bfloat16).reshape(2, chips, rows, piece)
+            theirs.append(swap(out[0]))
+            ours.append(out[1])
 
     def term(k, chip):
         return take(ours[k], chip).astype(jnp.float32) + take(theirs[k], chip).astype(jnp.float32)
@@ -102,9 +115,7 @@
         first = term(k, chip_behind(step, 1)).astype(jnp.bfloat16)
         first, held[k] = lax.optimization_barrier((first, held[k]))
         sums.append(first)
-    scale = 1.0 / math.sqrt(grad_rows.shape[0])
-    weight_grad = jnp.zeros((width, grad_rows.shape[1]), jnp.float32)
-    tn = (((0,), (0,)), ((), ()))
+    others = []
     for s in range(1, chips):
         for k, (_, step) in enumerate(chains):
             total = shift(sums[k], step).astype(jnp.float32)
@@ -112,13 +123,16 @@
             if s == chips - 1:
                 total = total + 0.5 * own[k].astype(jnp.float32)
             sums[k] = total.astype(jnp.bfloat16)
-        if s <= len(chains):
-            k = s - 1
-            sums[k], block = lax.optimization_barrier((sums[k], gathered[k]))
-            block = lax.dot_general(
-                block.reshape(n * rows, piece), grad_rows, tn, preferred_element_type=jnp.float32
-            )
+        k = s - 2
+        if 0 <= k < count:
+            sums[k], block = lax.optimization_barrier((sums[k], others[k]))
+            block = gathered[k].at[0].set(block).reshape(n * rows, piece)
+            block = lax.dot_general(block, ordered, tn, preferred_element_type=jnp.float32)
             weight_grad = lax.dynamic_update_slice(weight_grad, block * scale, (chains[k][0], 0))
+        k = s - 1
+        if k < count:
+            sums[k], mine = lax.optimization_barrier((sums[k], gathered[k][1]))
+            others.append(swap(mine))
     hidden_grad = jnp.concatenate(sums, axis=1)
     return (hidden_grad, weight_grad)
 

time: 613 us -> 447 us (0.73)
  waiting for transfers between devices: 281 us -> 95 us
  local copies, waits for them, and re-layouts: 78 us -> 121 us
  matrix products: 110 us -> 95 us
  between operations: 10.4 us -> 1.53 us
    ppermute x56, waiting for transfers between devices: 246 us -> 95 us  [shift(): return lax.ppermute(value, 'fsdp', pairs)]
    dynamic_update_slice x66 -> x2, local copies, waits for them, and re-layouts: 41.3 us -> 1.44 us  [put(): lax.dynamic_update_slice(into, block[None], start, allow_negative_indices...]
    ppermute x36 -> x8, waiting for transfers between devices: 35.3 us -> 0.02 us  [swap(): return lax.ppermute(value, 'fsdp', [(i, i ^ 1) for i in range(n)])]
    slice x0 -> x4, local copies, waits for them, and re-layouts: none -> 25.9 us  [local(): ours.append(out[1])]
    dynamic_update_slice x1 -> x32, local copies, waits for them, and re-layouts: 21.2 us -> 45 us  [keep(): lax.dynamic_update_slice(into, block[None, None], (1, chip, 0, 0), allow_...]
    broadcast_in_dim x0 -> x1, local copies, waits for them, and re-layouts: none -> 17.8 us  [local(): weight_grad = jnp.zeros((width, ordered.shape[1]), jnp.float32)]
    dot_general x12 -> x8, matrix products: 110 us -> 95 us  [the longest x4 50.5 us: local(): lax.dot_general(rows_now, weight[first:first + piece], nt, preferred_elem...]
    squeeze x0 -> x4, local copies, waits for them, and re-layouts: none -> 8.22 us  [local(): sums[k], mine = lax.optimization_barrier((sums[k], gathered[k][1]))]
  transfers between devices with their start and end apart: 93 -> 65, of which waited for: 49 -> 20; matrix products, arithmetic and copies ran while one was open for 39% -> 59% of each run, Pallas kernels for 0% -> 0%
where the time goes in v2:
time: 447 us; the launch traced here: 438 us
  local copies, waits for them, and re-layouts  121 us (27%)
  waiting for transfers between devices  95 us (21%)
  matrix products  95 us (21%)
  starting transfers between devices  64.8 us (14%)
  other arithmetic  60.5 us (14%)
    ppermute x56, waiting for transfers between devices, shift(): return lax.ppermute(value, 'fsdp', pairs)  95 us
    ppermute x56, starting transfers between devices, shift(): return lax.ppermute(value, 'fsdp', pairs)  62.9 us
    dot_general x4, matrix products, local(): lax.dot_general(rows_now, weight[first:first + piece], nt, preferred_elem...  50.5 us
    convert_element_type x25, other arithmetic, local(): sums[k] = total.astype(jnp.bfloat16)  50.5 us
    dynamic_update_slice x32, local copies, waits for them, and re-layouts, keep(): lax.dynamic_update_slice(into, block[None, None], (1, chip, 0, 0), allow_...  45 us
    dot_general x4, matrix products, local(): lax.dot_general(block, ordered, tn, preferred_element_type=jnp.float32)  44.5 us
    slice x4, local copies, waits for them, and re-layouts, local(): ours.append(out[1])  25.9 us
    broadcast_in_dim x1, local copies, waits for them, and re-layouts, local(): weight_grad = jnp.zeros((width, ordered.shape[1]), jnp.float32)  17.8 us
  transfers between devices with their start and end apart: 65, of which 20 were waited for; matrix products, arithmetic and copies ran while one was open for 59% of the time, Pallas kernels for 0%

profile of v2, /device:TPU:0, one launch (start us, length us, event | category | flops | bytes accessed | tf_op | source)
XLA Modules:
  0.0 438.2 jit_solution(5201489128511522123)
XLA Ops:
  0.6 2.7 fusion.48
  3.4 3.0 collective-permute-start
  16.1 1.9 copy-done.5
  18.0 2.9 copy-done.2
  24.7 5.4 %collective-permute-done.49 = bf16[64,3328]{1,0:T(8,128)(2,1)} collective-permute-done((bf16[64,3328]{1,0:T(8,128)(2,1)}, bf16[64,3328]{1,0:T(8,128)(2,1)}, u32[]{:S(2)}, u32[]{:S(2)}) %collective-permute-start.49) | collective-permute-done | bytes 426016 | tf_op jit(solution)/shard_map/ppermute | solution.py:52
  30.6 2.5 bitcast_dynamic-update-slice_fusion.28
  33.1 2.5 bitcast_dynamic-update-slice_fusion.12
  38.6 2.4 bitcast_dynamic-update-slice_fusion.20
  41.4 6.9 %collective-permute-done.50 = bf16[64,3328]{1,0:T(8,128)(2,1)} collective-permute-done((bf16[64,3328]{1,0:T(8,128)(2,1)}, bf16[64,3328]{1,0:T(8,128)(2,1)}, u32[]{:S(2)}, u32[]{:S(2)}) %collective-permute-start.50) | collective-permute-done | bytes 426016 | tf_op jit(solution)/shard_map/ppermute | solution.py:52
  48.8 2.4 bitcast_dynamic-update-slice_fusion.27
  51.3 2.4 bitcast_dynamic-update-slice_fusion.11
  55.2 2.4 bitcast_dynamic-update-slice_fusion.19
  57.6 2.4 bitcast_dynamic-update-slice_fusion.35
  64.4 12.2 %convolution_convert_fusion.3 = bf16[1024,3328]{1,0:T(8,128)(2,1)} fusion(bf16[1024,1024]{1,0:T(8,128)(2,1)S(1)} %bitcast.319, bf16[13312,1024]{1,0:T(8,128)(2,1)} %param.14), kind=kOutput, calls=%fused_computation.11 | convolution fusion | flops 6982729728 | bytes 15728640 | tf_op jit(solution)/shard_map/dot_general | solution.py:103
  76.6 7.0 %fusion.44 = (bf16[512,3328]{1,0:T(8,128)(2,1)}, bf16[512,3328]{1,0:T(8,128)(2,1)}) fusion(bf16[1024,3328]{1,0:T(8,128)(2,1)} %convolution_convert_fusion.3), kind=kLoop, calls=%fused_computation.131 | loop fusion | bytes 13631488 | tf_op jit(solution)/shard_map/slice | solution.py:108
  84.7 13.3 %convolution_convert_fusion.2 = bf16[1024,3328]{1,0:T(8,128)(2,1)} fusion(bf16[1024,1024]{1,0:T(8,128)(2,1)} %bitcast.320, bf16[13312,1024]{1,0:T(8,128)(2,1)} %param.14), kind=kOutput, calls=%fused_computation.10 | convolution fusion | flops 6982729728 | bytes 15728640 | tf_op jit(solution)/shard_map/dot_general | solution.py:103
  98.0 6.2 %fusion.45 = (bf16[512,3328]{1,0:T(8,128)(2,1)}, bf16[512,3328]{1,0:T(8,128)(2,1)}) fusion(bf16[1024,3328]{1,0:T(8,128)(2,1)} %convolution_convert_fusion.2), kind=kLoop, calls=%fused_computation.132 | loop fusion | bytes 13631488 | tf_op jit(solution)/shard_map/slice | solution.py:108
  106.1 2.5 bitcast_dynamic-update-slice_fusion.10
  113.8 9.9 %collective-permute-done.36 = bf16[64,3328]{1,0:T(8,128)(2,1)} collective-permute-done((bf16[64,3328]{1,0:T(8,128)(2,1)}, bf16[64,3328]{1,0:T(8,128)(2,1)}, u32[]{:S(2)}, u32[]{:S(2)}) %collective-permute-start.36) | collective-permute-done | bytes 426016 | tf_op jit(solution)/shard_map/ppermute | solution.py:52
  124.5 12.5 %convolution_convert_fusion.1 = bf16[1024,3328]{1,0:T(8,128)(2,1)} fusion(bf16[1024,1024]{1,0:T(8,128)(2,1)} %bitcast.321, bf16[13312,1024]{1,0:T(8,128)(2,1)} %param.14), kind=kOutput, calls=%fused_computation.9 | convolution fusion | flops 6982729728 | bytes 15728640 | tf_op jit(solution)/shard_map/dot_general | solution.py:103
  137.0 6.3 %fusion.46 = (bf16[512,3328]{1,0:T(8,128)(2,1)}, bf16[512,3328]{1,0:T(8,128)(2,1)}) fusion(bf16[1024,3328]{1,0:T(8,128)(2,1)} %convolution_convert_fusion.1), kind=kLoop, calls=%fused_computation.133 | loop fusion | bytes 13631488 | tf_op jit(solution)/shard_map/slice | solution.py:108
  143.3 2.5 bitcast_dynamic-update-slice_fusion.9
  149.5 8.8 %collective-permute-done.53 = bf16[64,3328]{1,0:T(8,128)(2,1)} collective-permute-done((bf16[64,3328]{1,0:T(8,128)(2,1)}, bf16[64,3328]{1,0:T(8,128)(2,1)}, u32[]{:S(2)}, u32[]{:S(2)}) %collective-permute-start.53) | collective-permute-done | bytes 426016 | tf_op jit(solution)/shard_map/ppermute | solution.py:52
  159.7 12.5 %convolution_convert_fusion = bf16[1024,3328]{1,0:T(8,128)(2,1)} fusion(bf16[1024,1024]{1,0:T(8,128)(2,1)} %bitcast.322, bf16[13312,1024]{1,0:T(8,128)(2,1)} %param.14), kind=kOutput, calls=%fused_computation.8 | convolution fusion | flops 6982729728 | bytes 15728640 | tf_op jit(solution)/shard_map/dot_general | solution.py:103
  172.2 6.3 %fusion.47 = (bf16[512,3328]{1,0:T(8,128)(2,1)}, bf16[512,3328]{1,0:T(8,128)(2,1)}) fusion(bf16[1024,3328]{1,0:T(8,128)(2,1)} %convolution_convert_fusion), kind=kLoop, calls=%fused_computation.134 | loop fusion | bytes 13631488 | tf_op jit(solution)/shard_map/slice | solution.py:108
  178.5 2.9 bitcast_dynamic-update-slice_fusion.8
  183.1 2.4 bitcast_dynamic-update-slice_fusion.7
  186.2 2.6 fusion.40
  190.3 2.7 fusion.41
  193.0 5.0 %collective-permute-done.5 = bf16[64,3328]{1,0:T(8,128)(2,1)S(1)} collective-permute-done((bf16[64,3328]{1,0:T(8,128)(2,1)}, bf16[64,3328]{1,0:T(8,128)(2,1)S(1)}, u32[]{:S(2)}, u32[]{:S(2)}) %collective-permute-start.5) | collective-permute-done | bytes 426016 | tf_op jit(solution)/shard_map/ppermute | solution.py:52
  204.6 6.1 %collective-permute-done.6 = bf16[64,3328]{1,0:T(8,128)(2,1)S(1)} collective-permute-done((bf16[64,3328]{1,0:T(8,128)(2,1)S(1)}, bf16[64,3328]{1,0:T(8,128)(2,1)S(1)}, u32[]{:S(2)}, u32[]{:S(2)}) %collective-permute-start.6) | collective-permute-done | bytes 426016 | tf_op jit(solution)/shard_map/ppermute | solution.py:52
  215.7 4.1 collective-permute-done.39
  222.7 6.2 %collective-permute-done.7 = bf16[64,3328]{1,0:T(8,128)(2,1)S(1)} collective-permute-done((bf16[64,3328]{1,0:T(8,128)(2,1)S(1)}, bf16[64,3328]{1,0:T(8,128)(2,1)S(1)}, u32[]{:S(2)}, u32[]{:S(2)}) %collective-permute-start.7) | collective-permute-done | bytes 426016 | tf_op jit(solution)/shard_map/ppermute | solution.py:52
  232.5 1.9 slice_bitcast_fusion.2
  237.4 4.0 slice_bitcast_fusion
  242.5 2.0 slice_bitcast_fusion.1
  244.6 2.6 collective-permute-done.8
  248.8 1.9 fusion.31
  258.8 6.6 %collective-permute-done.9 = bf16[64,3328]{1,0:T(8,128)(2,1)S(1)} collective-permute-done((bf16[64,3328]{1,0:T(8,128)(2,1)}, bf16[64,3328]{1,0:T(8,128)(2,1)S(1)}, u32[]{:S(2)}, u32[]{:S(2)}) %collective-permute-start.9) | collective-permute-done | bytes 426016 | tf_op jit(solution)/shard_map/ppermute | solution.py:52
  265.4 1.9 fusion.39
  268.1 2.0 fusion.30
  271.6 1.9 fusion.14
  277.9 4.5 %collective-permute-done.10 = bf16[64,3328]{1,0:T(8,128)(2,1)S(1)} collective-permute-done((bf16[64,3328]{1,0:T(8,128)(2,1)S(1)}, bf16[64,3328]{1,0:T(8,128)(2,1)S(1)}, u32[]{:S(2)}, u32[]{:S(2)}) %collective-permute-start.10) | collective-permute-done | bytes 426016 | tf_op jit(solution)/shard_map/ppermute | solution.py:52
  283.1 2.6 fusion.38
  285.8 5.7 %collective-permute-done.59 = bf16[64,3328]{1,0:T(8,128)(2,1)S(1)} collective-permute-done((bf16[64,3328]{1,0:T(8,128)(2,1)S(1)}, bf16[64,3328]{1,0:T(8,128)(2,1)S(1)}, u32[]{:S(2)}, u32[]{:S(2)}) %collective-permute-start.59) | collective-permute-done | bytes 426016 | tf_op jit(solution)/shard_map/ppermute | solution.py:52
  291.5 1.9 fusion.13
  297.3 2.8 fusion.29
  300.0 4.8 %collective-permute-done.60 = bf16[64,3328]{1,0:T(8,128)(2,1)S(1)} collective-permute-done((bf16[64,3328]{1,0:T(8,128)(2,1)S(1)}, bf16[64,3328]{1,0:T(8,128)(2,1)S(1)}, u32[]{:S(2)}, u32[]{:S(2)}) %collective-permute-start.60) | collective-permute-done | bytes 426016 | tf_op jit(solution)/shard_map/ppermute | solution.py:52
  307.9 2.6 fusion.20
  310.5 6.6 %collective-permute-done.61 = bf16[64,3328]{1,0:T(8,128)(2,1)S(1)} collective-permute-done((bf16[64,3328]{1,0:T(8,128)(2,1)S(1)}, bf16[64,3328]{1,0:T(8,128)(2,1)S(1)}, u32[]{:S(2)}, u32[]{:S(2)}) %collective-permute-start.61) | collective-permute-done | bytes 426016 | tf_op jit(solution)/shard_map/ppermute | solution.py:52
  320.9 17.8 %broadcast_in_dim.108 = f32[13312,1024]{1,0:T(8,128)} broadcast(f32[]{:T(128)} %constant.119.clone.1), dimensions={} | broadcast | bytes 54525956 | tf_op jit(solution)/shard_map/broadcast_in_dim | solution.py:75
  338.7 12.2 %fusion.3 = f32[13312,1024]{1,0:T(8,128)} fusion(f32[13312,1024]{1,0:T(8,128)} %broadcast_in_dim.108, bf16[2,8,64,3328]{3,2,1,0:T(8,128)(2,1)S(1)} %bitcast_dynamic-update-slice_fusion.3, bf16[1,8,64,1024]{3,2,1,0:T(8,128)(2,1)} %copy-done.12, bf16[1,8,64,1024]{3,2,1,0:T(8,128)(2,1)} %copy-done.10), kind=kOutput, calls=%fused_computation.7 | convolution fusion | flops 6983778304 | bytes 22544384 | tf_op jit(solution)/shard_map/dot_general | solution.py:130
  351.5 2.2 bitcast_dynamic-update-slice_fusion.2
  353.8 10.8 %fusion.2 = f32[13312,1024]{1,0:T(8,128)} fusion(f32[13312,1024]{1,0:T(8,128)} %fusion.3, bf16[2,8,64,3328]{3,2,1,0:T(8,128)(2,1)S(1)} %bitcast_dynamic-update-slice_fusion.2, bf16[1,8,64,1024]{3,2,1,0:T(8,128)(2,1)S(1)} %copy-done.13, bf16[1,8,64,1024]{3,2,1,0:T(8,128)(2,1)S(1)} %copy-done.11), kind=kOutput, calls=%fused_computation.5 | convolution fusion | flops 6983778304 | bytes 22544384 | tf_op jit(solution)/shard_map/dot_general | solution.py:130
  364.6 1.9 fusion.37
  372.0 2.4 bitcast_dynamic-update-slice_fusion.1
  374.3 10.8 %fusion.1 = f32[13312,1024]{1,0:T(8,128)} fusion(f32[13312,1024]{1,0:T(8,128)} %fusion.2, bf16[2,8,64,3328]{3,2,1,0:T(8,128)(2,1)S(1)} %bitcast_dynamic-update-slice_fusion.1, bf16[1,8,64,1024]{3,2,1,0:T(8,128)(2,1)S(1)} %copy-done.13, bf16[1,8,64,1024]{3,2,1,0:T(8,128)(2,1)S(1)} %copy-done.11), kind=kOutput, calls=%fused_computation.3 | convolution fusion | flops 6983778304 | bytes 22544384 | tf_op jit(solution)/shard_map/dot_general | solution.py:130
  391.3 1.9 fusion.19
  394.9 2.2 bitcast_dynamic-update-slice_fusion
  405.5 6.8 %collective-permute-done.63 = bf16[64,3328]{1,0:T(8,128)(2,1)S(1)} collective-permute-done((bf16[64,3328]{1,0:T(8,128)(2,1)S(1)}, bf16[64,3328]{1,0:T(8,128)(2,1)S(1)}, u32[]{:S(2)}, u32[]{:S(2)}) %collective-permute-start.63) | collective-permute-done | bytes 426016 | tf_op jit(solution)/shard_map/ppermute | solution.py:52
  412.3 1.9 fusion.10
  414.7 1.9 fusion.18
  421.9 10.8 %fusion = f32[13312,1024]{1,0:T(8,128)} fusion(f32[13312,1024]{1,0:T(8,128)} %fusion.1, bf16[2,8,64,3328]{3,2,1,0:T(8,128)(2,1)S(1)} %bitcast_dynamic-update-slice_fusion, bf16[1,8,64,1024]{3,2,1,0:T(8,128)(2,1)S(1)} %copy-done.13, bf16[1,8,64,1024]{3,2,1,0:T(8,128)(2,1)S(1)} %copy-done.11), kind=kOutput, calls=%fused_computation.1 | convolution fusion | flops 6983778304 | bytes 22544384 | tf_op jit(solution)/shard_map/dot_general | solution.py:130
  432.7 4.0 fusion.33
  (219 shorter events, 121.1 us)
Async XLA Ops:
  3.4 19.2 %collective-permute-start = (bf16[64,3328]{1,0:T(8,128)(2,1)}, bf16[64,3328]{1,0:T(8,128)(2,1)S(1)}, u32[]{:S(2)}, u32[]{:S(2)}) collective-permute-start(bf16[64,3328]{1,0:T(8,128)(2,1)} %get-tuple-element.140), channel_id=1, source_target_pairs={{0,8},{2,10},{8,16},{10,18},{16,24},{18,26},{24,28},{26,30},{28,20... | collective-permute-start | bytes 1277960 | tf_op jit(solution)/shard_map/ppermute | solution.py:52
  6.4 53.5 %collective-permute-start.2 = (bf16[512,1024]{1,0:T(8,128)(2,1)}, bf16[512,1024]{1,0:T(8,128)(2,1)}, u32[]{:S(2)}, u32[]{:S(2)}) collective-permute-start(bf16[512,1024]{1,0:T(8,128)(2,1)} %param.13), channel_id=1, source_target_pairs={{0,1},{1,0},{2,3},{3,2},{4,5},{5,4},{6,7},{7,6},{8,9},{9,8},{10,11... | collective-permute-start | bytes 3145736 | tf_op jit(solution)/shard_map/ppermute | solution.py:66
  7.9 16.3 %collective-permute-start.17 = (bf16[64,3328]{1,0:T(8,128)(2,1)}, bf16[64,3328]{1,0:T(8,128)(2,1)}, u32[]{:S(2)}, u32[]{:S(2)}) collective-permute-start(bf16[64,3328]{1,0:T(8,128)(2,1)} %get-tuple-element.141), channel_id=1, source_target_pairs={{0,4},{2,6},{8,0},{10,2},{16,8},{18,10},{24,16},{26,18},{28,24},{3... | collective-permute-start | bytes 1277960 | tf_op jit(solution)/shard_map/ppermute | solution.py:52
  8.4 21.8 %collective-permute-start.49 = (bf16[64,3328]{1,0:T(8,128)(2,1)}, bf16[64,3328]{1,0:T(8,128)(2,1)}, u32[]{:S(2)}, u32[]{:S(2)}) collective-permute-start(bf16[64,3328]{1,0:T(8,128)(2,1)} %get-tuple-element.142), channel_id=1, source_target_pairs={{0,4},{2,6},{8,0},{10,2},{16,8},{18,10},{24,16},{26,18},{28,24},{3... | collective-permute-start | bytes 1277960 | tf_op jit(solution)/shard_map/ppermute | solution.py:52
  9.9 25.7 %collective-permute-start.33 = (bf16[64,3328]{1,0:T(8,128)(2,1)}, bf16[64,3328]{1,0:T(8,128)(2,1)}, u32[]{:S(2)}, u32[]{:S(2)}) collective-permute-start(bf16[64,3328]{1,0:T(8,128)(2,1)} %get-tuple-element.143), channel_id=1, source_target_pairs={{0,8},{2,10},{8,16},{10,18},{16,24},{18,26},{24,28},{26,30},{28,20... | collective-permute-start | bytes 1277960 | tf_op jit(solution)/shard_map/ppermute | solution.py:52
  22.6 35.0 %collective-permute-start.1 = (bf16[64,3328]{1,0:T(8,128)(2,1)S(1)}, bf16[64,3328]{1,0:T(8,128)(2,1)}, u32[]{:S(2)}, u32[]{:S(2)}) collective-permute-start(bf16[64,3328]{1,0:T(8,128)(2,1)S(1)} %collective-permute-done), channel_id=1, source_target_pairs={{0,8},{2,10},{8,16},{10,18},{16,24},{18,26},{24,28},{26,30},{28,20... | collective-permute-start | bytes 1277960 | tf_op jit(solution)/shard_map/ppermute | solution.py:52
  24.2 16.7 %collective-permute-start.18 = (bf16[64,3328]{1,0:T(8,128)(2,1)}, bf16[64,3328]{1,0:T(8,128)(2,1)}, u32[]{:S(2)}, u32[]{:S(2)}) collective-permute-start(bf16[64,3328]{1,0:T(8,128)(2,1)} %collective-permute-done.17), channel_id=1, source_target_pairs={{0,4},{2,6},{8,0},{10,2},{16,8},{18,10},{24,16},{26,18},{28,24},{3... | collective-permute-start | bytes 1277960 | tf_op jit(solution)/shard_map/ppermute | solution.py:52
  30.1 18.3 %collective-permute-start.50 = (bf16[64,3328]{1,0:T(8,128)(2,1)}, bf16[64,3328]{1,0:T(8,128)(2,1)}, u32[]{:S(2)}, u32[]{:S(2)}) collective-permute-start(bf16[64,3328]{1,0:T(8,128)(2,1)} %collective-permute-done.49), channel_id=1, source_target_pairs={{0,4},{2,6},{8,0},{10,2},{16,8},{18,10},{24,16},{26,18},{28,24},{3... | collective-permute-start | bytes 1277960 | tf_op jit(solution)/shard_map/ppermute | solution.py:52
  35.6 18.1 %collective-permute-start.34 = (bf16[64,3328]{1,0:T(8,128)(2,1)}, bf16[64,3328]{1,0:T(8,128)(2,1)}, u32[]{:S(2)}, u32[]{:S(2)}) collective-permute-start(bf16[64,3328]{1,0:T(8,128)(2,1)} %collective-permute-done.33), channel_id=1, source_target_pairs={{0,8},{2,10},{8,16},{10,18},{16,24},{18,26},{24,28},{26,30},{28,20... | collective-permute-start | bytes 1277960 | tf_op jit(solution)/shard_map/ppermute | solution.py:52
  41.0 42.7 %collective-permute-start.19 = (bf16[64,3328]{1,0:T(8,128)(2,1)}, bf16[64,3328]{1,0:T(8,128)(2,1)}, u32[]{:S(2)}, u32[]{:S(2)}) collective-permute-start(bf16[64,3328]{1,0:T(8,128)(2,1)} %collective-permute-done.18), channel_id=1, source_target_pairs={{0,4},{2,6},{8,0},{10,2},{16,8},{18,10},{24,16},{26,18},{28,24},{3... | collective-permute-start | bytes 1277960 | tf_op jit(solution)/shard_map/ppermute | solution.py:52
  48.4 57.6 %collective-permute-start.51 = (bf16[64,3328]{1,0:T(8,128)(2,1)}, bf16[64,3328]{1,0:T(8,128)(2,1)}, u32[]{:S(2)}, u32[]{:S(2)}) collective-permute-start(bf16[64,3328]{1,0:T(8,128)(2,1)} %collective-permute-done.50), channel_id=1, source_target_pairs={{0,4},{2,6},{8,0},{10,2},{16,8},{18,10},{24,16},{26,18},{28,24},{3... | collective-permute-start | bytes 1277960 | tf_op jit(solution)/shard_map/ppermute | solution.py:52
  53.7 54.9 %collective-permute-start.35 = (bf16[64,3328]{1,0:T(8,128)(2,1)}, bf16[64,3328]{1,0:T(8,128)(2,1)}, u32[]{:S(2)}, u32[]{:S(2)}) collective-permute-start(bf16[64,3328]{1,0:T(8,128)(2,1)} %collective-permute-done.34), channel_id=1, source_target_pairs={{0,8},{2,10},{8,16},{10,18},{16,24},{18,26},{24,28},{26,30},{28,20... | collective-permute-start | bytes 1277960 | tf_op jit(solution)/shard_map/ppermute | solution.py:52
  62.9 48.6 %collective-permute-start.3 = (bf16[64,3328]{1,0:T(8,128)(2,1)}, bf16[64,3328]{1,0:T(8,128)(2,1)}, u32[]{:S(2)}, u32[]{:S(2)}) collective-permute-start(bf16[64,3328]{1,0:T(8,128)(2,1)} %collective-permute-done.1), channel_id=1, source_target_pairs={{0,8},{2,10},{8,16},{10,18},{16,24},{18,26},{24,28},{26,30},{28,20... | collective-permute-start | bytes 1277960 | tf_op jit(solution)/shard_map/ppermute | solution.py:52
  83.7 101.8 %collective-permute-start.4 = (bf16[8,64,3328]{2,1,0:T(8,128)(2,1)}, bf16[8,64,3328]{2,1,0:T(8,128)(2,1)}, u32[]{:S(2)}, u32[]{:S(2)}) collective-permute-start(bf16[8,64,3328]{2,1,0:T(8,128)(2,1)} %bitcast.315), channel_id=1, source_target_pairs={{0,2},{2,0},{4,6},{6,4},{8,10},{10,8},{12,14},{14,12},{16,18},{18,... | collective-permute-start | bytes 10223624 | tf_op jit(solution)/shard_map/ppermute | solution.py:55
  83.7 62.1 %collective-permute-start.20 = (bf16[64,3328]{1,0:T(8,128)(2,1)}, bf16[64,3328]{1,0:T(8,128)(2,1)S(1)}, u32[]{:S(2)}, u32[]{:S(2)}) collective-permute-start(bf16[64,3328]{1,0:T(8,128)(2,1)} %collective-permute-done.19), channel_id=1, source_target_pairs={{0,4},{2,6},{8,0},{10,2},{16,8},{18,10},{24,16},{26,18},{28,24},{3... | collective-permute-start | bytes 1277960 | tf_op jit(solution)/shard_map/ppermute | solution.py:52
  106.0 82.9 %collective-permute-start.21 = (bf16[8,64,3328]{2,1,0:T(8,128)(2,1)}, bf16[8,64,3328]{2,1,0:T(8,128)(2,1)}, u32[]{:S(2)}, u32[]{:S(2)}) collective-permute-start(bf16[8,64,3328]{2,1,0:T(8,128)(2,1)} %bitcast.316), channel_id=1, source_target_pairs={{0,2},{2,0},{4,6},{6,4},{8,10},{10,8},{12,14},{14,12},{16,18},{18,... | collective-permute-start | bytes 10223624 | tf_op jit(solution)/shard_map/ppermute | solution.py:55
  108.5 34.8 %collective-permute-start.52 = (bf16[64,3328]{1,0:T(8,128)(2,1)}, bf16[64,3328]{1,0:T(8,128)(2,1)}, u32[]{:S(2)}, u32[]{:S(2)}) collective-permute-start(bf16[64,3328]{1,0:T(8,128)(2,1)} %collective-permute-done.51), channel_id=1, source_target_pairs={{0,4},{2,6},{8,0},{10,2},{16,8},{18,10},{24,16},{26,18},{28,24},{3... | collective-permute-start | bytes 1277960 | tf_op jit(solution)/shard_map/ppermute | solution.py:52
  111.5 12.3 %collective-permute-start.36 = (bf16[64,3328]{1,0:T(8,128)(2,1)}, bf16[64,3328]{1,0:T(8,128)(2,1)}, u32[]{:S(2)}, u32[]{:S(2)}) collective-permute-start(bf16[64,3328]{1,0:T(8,128)(2,1)} %collective-permute-done.35), channel_id=1, source_target_pairs={{0,8},{2,10},{8,16},{10,18},{16,24},{18,26},{24,28},{26,30},{28,20... | collective-permute-start | bytes 1277960 | tf_op jit(solution)/shard_map/ppermute | solution.py:52
  123.8 57.6 %collective-permute-start.37 = (bf16[64,3328]{1,0:T(8,128)(2,1)}, bf16[64,3328]{1,0:T(8,128)(2,1)}, u32[]{:S(2)}, u32[]{:S(2)}) collective-permute-start(bf16[64,3328]{1,0:T(8,128)(2,1)} %collective-permute-done.36), channel_id=1, source_target_pairs={{0,8},{2,10},{8,16},{10,18},{16,24},{18,26},{24,28},{26,30},{28,20... | collective-permute-start | bytes 1277960 | tf_op jit(solution)/shard_map/ppermute | solution.py:52
  143.3 56.0 %collective-permute-start.38 = (bf16[8,64,3328]{2,1,0:T(8,128)(2,1)}, bf16[8,64,3328]{2,1,0:T(8,128)(2,1)}, u32[]{:S(2)}, u32[]{:S(2)}) collective-permute-start(bf16[8,64,3328]{2,1,0:T(8,128)(2,1)} %bitcast.317), channel_id=1, source_target_pairs={{0,2},{2,0},{4,6},{6,4},{8,10},{10,8},{12,14},{14,12},{16,18},{18,... | collective-permute-start | bytes 10223624 | tf_op jit(solution)/shard_map/ppermute | solution.py:55
  145.8 12.5 %collective-permute-start.53 = (bf16[64,3328]{1,0:T(8,128)(2,1)}, bf16[64,3328]{1,0:T(8,128)(2,1)}, u32[]{:S(2)}, u32[]{:S(2)}) collective-permute-start(bf16[64,3328]{1,0:T(8,128)(2,1)} %collective-permute-done.52), channel_id=1, source_target_pairs={{0,4},{2,6},{8,0},{10,2},{16,8},{18,10},{24,16},{26,18},{28,24},{3... | collective-permute-start | bytes 1277960 | tf_op jit(solution)/shard_map/ppermute | solution.py:52
  158.4 24.7 %collective-permute-start.54 = (bf16[64,3328]{1,0:T(8,128)(2,1)}, bf16[64,3328]{1,0:T(8,128)(2,1)}, u32[]{:S(2)}, u32[]{:S(2)}) collective-permute-start(bf16[64,3328]{1,0:T(8,128)(2,1)} %collective-permute-done.53), channel_id=1, source_target_pairs={{0,4},{2,6},{8,0},{10,2},{16,8},{18,10},{24,16},{26,18},{28,24},{3... | collective-permute-start | bytes 1277960 | tf_op jit(solution)/shard_map/ppermute | solution.py:52
  181.3 30.8 %collective-permute-start.55 = (bf16[8,64,3328]{2,1,0:T(8,128)(2,1)}, bf16[8,64,3328]{2,1,0:T(8,128)(2,1)S(1)}, u32[]{:S(2)}, u32[]{:S(2)}) collective-permute-start(bf16[8,64,3328]{2,1,0:T(8,128)(2,1)} %bitcast.318), channel_id=1, source_target_pairs={{0,2},{2,0},{4,6},{6,4},{8,10},{10,8},{12,14},{14,12},{16,18},{18,... | collective-permute-start | bytes 10223624 | tf_op jit(solution)/shard_map/ppermute | solution.py:55
  185.5 12.4 %collective-permute-start.5 = (bf16[64,3328]{1,0:T(8,128)(2,1)}, bf16[64,3328]{1,0:T(8,128)(2,1)S(1)}, u32[]{:S(2)}, u32[]{:S(2)}) collective-permute-start(bf16[64,3328]{1,0:T(8,128)(2,1)} %collective-permute-done.3), channel_id=1, source_target_pairs={{0,8},{2,10},{8,16},{10,18},{16,24},{18,26},{24,28},{26,30},{28,20... | collective-permute-start | bytes 1277960 | tf_op jit(solution)/shard_map/ppermute | solution.py:52
  188.8 12.2 %collective-permute-start.22 = (bf16[64,3328]{1,0:T(8,128)(2,1)S(1)}, bf16[64,3328]{1,0:T(8,128)(2,1)S(1)}, u32[]{:S(2)}, u32[]{:S(2)}) collective-permute-start(bf16[64,3328]{1,0:T(8,128)(2,1)S(1)} %collective-permute-done.20), channel_id=1, source_target_pairs={{0,4},{2,6},{8,0},{10,2},{16,8},{18,10},{24,16},{26,18},{28,24},{3... | collective-permute-start | bytes 1277960 | tf_op jit(solution)/shard_map/ppermute | solution.py:52
  197.9 12.7 %collective-permute-start.6 = (bf16[64,3328]{1,0:T(8,128)(2,1)S(1)}, bf16[64,3328]{1,0:T(8,128)(2,1)S(1)}, u32[]{:S(2)}, u32[]{:S(2)}) collective-permute-start(bf16[64,3328]{1,0:T(8,128)(2,1)S(1)} %collective-permute-done.5), channel_id=1, source_target_pairs={{0,8},{2,10},{8,16},{10,18},{16,24},{18,26},{24,28},{26,30},{28,20... | collective-permute-start | bytes 1277960 | tf_op jit(solution)/shard_map/ppermute | solution.py:52
  199.3 20.4 %collective-permute-start.39 = (bf16[64,3328]{1,0:T(8,128)(2,1)}, bf16[64,3328]{1,0:T(8,128)(2,1)S(1)}, u32[]{:S(2)}, u32[]{:S(2)}) collective-permute-start(bf16[64,3328]{1,0:T(8,128)(2,1)} %collective-permute-done.37), channel_id=1, source_target_pairs={{0,8},{2,10},{8,16},{10,18},{16,24},{18,26},{24,28},{26,30},{28,20... | collective-permute-start | bytes 1277960 | tf_op jit(solution)/shard_map/ppermute | solution.py:52
  201.0 12.5 %collective-permute-start.23 = (bf16[64,3328]{1,0:T(8,128)(2,1)S(1)}, bf16[64,3328]{1,0:T(8,128)(2,1)S(1)}, u32[]{:S(2)}, u32[]{:S(2)}) collective-permute-start(bf16[64,3328]{1,0:T(8,128)(2,1)S(1)} %collective-permute-done.22), channel_id=1, source_target_pairs={{0,4},{2,6},{8,0},{10,2},{16,8},{18,10},{24,16},{26,18},{28,24},{3... | collective-permute-start | bytes 1277960 | tf_op jit(solution)/shard_map/ppermute | solution.py:52
  210.7 18.3 %collective-permute-start.7 = (bf16[64,3328]{1,0:T(8,128)(2,1)S(1)}, bf16[64,3328]{1,0:T(8,128)(2,1)S(1)}, u32[]{:S(2)}, u32[]{:S(2)}) collective-permute-start(bf16[64,3328]{1,0:T(8,128)(2,1)S(1)} %collective-permute-done.6), channel_id=1, source_target_pairs={{0,8},{2,10},{8,16},{10,18},{16,24},{18,26},{24,28},{26,30},{28,20... | collective-permute-start | bytes 1277960 | tf_op jit(solution)/shard_map/ppermute | solution.py:52
  212.1 22.3 %collective-permute-start.56 = (bf16[64,3328]{1,0:T(8,128)(2,1)}, bf16[64,3328]{1,0:T(8,128)(2,1)S(1)}, u32[]{:S(2)}, u32[]{:S(2)}) collective-permute-start(bf16[64,3328]{1,0:T(8,128)(2,1)} %collective-permute-done.54), channel_id=1, source_target_pairs={{0,4},{2,6},{8,0},{10,2},{16,8},{18,10},{24,16},{26,18},{28,24},{3... | collective-permute-start | bytes 1277960 | tf_op jit(solution)/shard_map/ppermute | solution.py:52
  213.5 17.0 %collective-permute-start.24 = (bf16[64,3328]{1,0:T(8,128)(2,1)S(1)}, bf16[64,3328]{1,0:T(8,128)(2,1)S(1)}, u32[]{:S(2)}, u32[]{:S(2)}) collective-permute-start(bf16[64,3328]{1,0:T(8,128)(2,1)S(1)} %collective-permute-done.23), channel_id=1, source_target_pairs={{0,4},{2,6},{8,0},{10,2},{16,8},{18,10},{24,16},{26,18},{28,24},{3... | collective-permute-start | bytes 1277960 | tf_op jit(solution)/shard_map/ppermute | solution.py:52
  219.8 21.6 %collective-permute-start.40 = (bf16[64,3328]{1,0:T(8,128)(2,1)S(1)}, bf16[64,3328]{1,0:T(8,128)(2,1)S(1)}, u32[]{:S(2)}, u32[]{:S(2)}) collective-permute-start(bf16[64,3328]{1,0:T(8,128)(2,1)S(1)} %collective-permute-done.39), channel_id=1, source_target_pairs={{0,8},{2,10},{8,16},{10,18},{16,24},{18,26},{24,28},{26,30},{28,20... | collective-permute-start | bytes 1277960 | tf_op jit(solution)/shard_map/ppermute | solution.py:52
  228.9 18.3 %collective-permute-start.8 = (bf16[64,3328]{1,0:T(8,128)(2,1)S(1)}, bf16[64,3328]{1,0:T(8,128)(2,1)S(1)}, u32[]{:S(2)}, u32[]{:S(2)}) collective-permute-start(bf16[64,3328]{1,0:T(8,128)(2,1)S(1)} %collective-permute-done.7), channel_id=1, source_target_pairs={{0,8},{2,10},{8,16},{10,18},{16,24},{18,26},{24,28},{26,30},{28,20... | collective-permute-start | bytes 1277960 | tf_op jit(solution)/shard_map/ppermute | solution.py:52
  230.5 18.3 %collective-permute-start.25 = (bf16[64,3328]{1,0:T(8,128)(2,1)}, bf16[64,3328]{1,0:T(8,128)(2,1)S(1)}, u32[]{:S(2)}, u32[]{:S(2)}) collective-permute-start(bf16[64,3328]{1,0:T(8,128)(2,1)} %fusion.41), channel_id=1, source_target_pairs={{0,4},{2,6},{8,0},{10,2},{16,8},{18,10},{24,16},{26,18},{28,24},{3... | collective-permute-start | bytes 1277960 | tf_op jit(solution)/shard_map/ppermute | solution.py:52
  234.4 17.7 %collective-permute-start.57 = (bf16[64,3328]{1,0:T(8,128)(2,1)}, bf16[64,3328]{1,0:T(8,128)(2,1)}, u32[]{:S(2)}, u32[]{:S(2)}) collective-permute-start(bf16[64,3328]{1,0:T(8,128)(2,1)} %fusion.43), channel_id=1, source_target_pairs={{0,4},{2,6},{8,0},{10,2},{16,8},{18,10},{24,16},{26,18},{28,24},{3... | collective-permute-start | bytes 1277960 | tf_op jit(solution)/shard_map/ppermute | solution.py:52
  241.4 14.9 %collective-permute-start.41 = (bf16[64,3328]{1,0:T(8,128)(2,1)S(1)}, bf16[64,3328]{1,0:T(8,128)(2,1)S(1)}, u32[]{:S(2)}, u32[]{:S(2)}) collective-permute-start(bf16[64,3328]{1,0:T(8,128)(2,1)S(1)} %fusion.42), channel_id=1, source_target_pairs={{0,8},{2,10},{8,16},{10,18},{16,24},{18,26},{24,28},{26,30},{28,20... | collective-permute-start | bytes 1277960 | tf_op jit(solution)/shard_map/ppermute | solution.py:52
  247.2 18.3 %collective-permute-start.9 = (bf16[64,3328]{1,0:T(8,128)(2,1)}, bf16[64,3328]{1,0:T(8,128)(2,1)S(1)}, u32[]{:S(2)}, u32[]{:S(2)}) collective-permute-start(bf16[64,3328]{1,0:T(8,128)(2,1)} %fusion.40), channel_id=1, source_target_pairs={{0,8},{2,10},{8,16},{10,18},{16,24},{18,26},{24,28},{26,30},{28,20... | collective-permute-start | bytes 1277960 | tf_op jit(solution)/shard_map/ppermute | solution.py:52
  250.7 17.3 %collective-permute-start.26 = (bf16[64,3328]{1,0:T(8,128)(2,1)S(1)}, bf16[64,3328]{1,0:T(8,128)(2,1)S(1)}, u32[]{:S(2)}, u32[]{:S(2)}) collective-permute-start(bf16[64,3328]{1,0:T(8,128)(2,1)S(1)} %fusion.31), channel_id=1, source_target_pairs={{0,4},{2,6},{8,0},{10,2},{16,8},{18,10},{24,16},{26,18},{28,24},{3... | collective-permute-start | bytes 1277960 | tf_op jit(solution)/shard_map/ppermute | solution.py:52
  253.9 17.5 %collective-permute-start.58 = (bf16[64,3328]{1,0:T(8,128)(2,1)S(1)}, bf16[64,3328]{1,0:T(8,128)(2,1)S(1)}, u32[]{:S(2)}, u32[]{:S(2)}) collective-permute-start(bf16[64,3328]{1,0:T(8,128)(2,1)S(1)} %fusion.15), channel_id=1, source_target_pairs={{0,4},{2,6},{8,0},{10,2},{16,8},{18,10},{24,16},{26,18},{28,24},{3... | collective-permute-start | bytes 1277960 | tf_op jit(solution)/shard_map/ppermute | solution.py:52
  258.0 16.5 %collective-permute-start.42 = (bf16[64,3328]{1,0:T(8,128)(2,1)S(1)}, bf16[64,3328]{1,0:T(8,128)(2,1)S(1)}, u32[]{:S(2)}, u32[]{:S(2)}) collective-permute-start(bf16[64,3328]{1,0:T(8,128)(2,1)S(1)} %fusion.23), channel_id=1, source_target_pairs={{0,8},{2,10},{8,16},{10,18},{16,24},{18,26},{24,28},{26,30},{28,20... | collective-permute-start | bytes 1277960 | tf_op jit(solution)/shard_map/ppermute | solution.py:52
  267.3 15.1 %collective-permute-start.10 = (bf16[64,3328]{1,0:T(8,128)(2,1)S(1)}, bf16[64,3328]{1,0:T(8,128)(2,1)S(1)}, u32[]{:S(2)}, u32[]{:S(2)}) collective-permute-start(bf16[64,3328]{1,0:T(8,128)(2,1)S(1)} %fusion.39), channel_id=1, source_target_pairs={{0,8},{2,10},{8,16},{10,18},{16,24},{18,26},{24,28},{26,30},{28,20... | collective-permute-start | bytes 1277960 | tf_op jit(solution)/shard_map/ppermute | solution.py:52
  268.1 50.9 %collective-permute-start.11 = (bf16[8,64,3328]{2,1,0:T(8,128)(2,1)S(1)}, bf16[8,64,3328]{2,1,0:T(8,128)(2,1)S(1)}, u32[]{:S(2)}, u32[]{:S(2)}) collective-permute-start(bf16[8,64,3328]{2,1,0:T(8,128)(2,1)S(1)} %slice_bitcast_fusion.3), channel_id=1, source_target_pairs={{0,2},{2,0},{4,6},{6,4},{8,10},{10,8},{12,14},{14,12},{16,18},{18,... | collective-permute-start | bytes 10223624 | tf_op jit(solution)/shard_map/ppermute | solution.py:55
  270.0 27.2 %collective-permute-start.27 = (bf16[64,3328]{1,0:T(8,128)(2,1)S(1)}, bf16[64,3328]{1,0:T(8,128)(2,1)S(1)}, u32[]{:S(2)}, u32[]{:S(2)}) collective-permute-start(bf16[64,3328]{1,0:T(8,128)(2,1)S(1)} %fusion.30), channel_id=1, source_target_pairs={{0,4},{2,6},{8,0},{10,2},{16,8},{18,10},{24,16},{26,18},{28,24},{3... | collective-permute-start | bytes 1277960 | tf_op jit(solution)/shard_map/ppermute | solution.py:52
  271.4 79.5 %collective-permute-start.28 = (bf16[8,64,3328]{2,1,0:T(8,128)(2,1)}, bf16[8,64,3328]{2,1,0:T(8,128)(2,1)}, u32[]{:S(2)}, u32[]{:S(2)}) collective-permute-start(bf16[8,64,3328]{2,1,0:T(8,128)(2,1)} %slice_bitcast_fusion.2), channel_id=1, source_target_pairs={{0,2},{2,0},{4,6},{6,4},{8,10},{10,8},{12,14},{14,12},{16,18},{18,... | collective-permute-start | bytes 10223624 | tf_op jit(solution)/shard_map/ppermute | solution.py:55
  274.6 16.9 %collective-permute-start.59 = (bf16[64,3328]{1,0:T(8,128)(2,1)S(1)}, bf16[64,3328]{1,0:T(8,128)(2,1)S(1)}, u32[]{:S(2)}, u32[]{:S(2)}) collective-permute-start(bf16[64,3328]{1,0:T(8,128)(2,1)S(1)} %fusion.14), channel_id=1, source_target_pairs={{0,4},{2,6},{8,0},{10,2},{16,8},{18,10},{24,16},{26,18},{28,24},{3... | collective-permute-start | bytes 1277960 | tf_op jit(solution)/shard_map/ppermute | solution.py:52
  282.4 12.3 %collective-permute-start.43 = (bf16[64,3328]{1,0:T(8,128)(2,1)S(1)}, bf16[64,3328]{1,0:T(8,128)(2,1)S(1)}, u32[]{:S(2)}, u32[]{:S(2)}) collective-permute-start(bf16[64,3328]{1,0:T(8,128)(2,1)S(1)} %fusion.22), channel_id=1, source_target_pairs={{0,8},{2,10},{8,16},{10,18},{16,24},{18,26},{24,28},{26,30},{28,20... | collective-permute-start | bytes 1277960 | tf_op jit(solution)/shard_map/ppermute | solution.py:52
  293.3 11.5 %collective-permute-start.60 = (bf16[64,3328]{1,0:T(8,128)(2,1)S(1)}, bf16[64,3328]{1,0:T(8,128)(2,1)S(1)}, u32[]{:S(2)}, u32[]{:S(2)}) collective-permute-start(bf16[64,3328]{1,0:T(8,128)(2,1)S(1)} %fusion.13), channel_id=1, source_target_pairs={{0,4},{2,6},{8,0},{10,2},{16,8},{18,10},{24,16},{26,18},{28,24},{3... | collective-permute-start | bytes 1277960 | tf_op jit(solution)/shard_map/ppermute | solution.py:52
  296.5 11.4 %collective-permute-start.44 = (bf16[64,3328]{1,0:T(8,128)(2,1)S(1)}, bf16[64,3328]{1,0:T(8,128)(2,1)S(1)}, u32[]{:S(2)}, u32[]{:S(2)}) collective-permute-start(bf16[64,3328]{1,0:T(8,128)(2,1)S(1)} %fusion.21), channel_id=1, source_target_pairs={{0,8},{2,10},{8,16},{10,18},{16,24},{18,26},{24,28},{26,30},{28,20... | collective-permute-start | bytes 1277960 | tf_op jit(solution)/shard_map/ppermute | solution.py:52
  297.3 73.1 %collective-permute-start.45 = (bf16[8,64,3328]{2,1,0:T(8,128)(2,1)}, bf16[8,64,3328]{2,1,0:T(8,128)(2,1)}, u32[]{:S(2)}, u32[]{:S(2)}) collective-permute-start(bf16[8,64,3328]{2,1,0:T(8,128)(2,1)} %slice_bitcast_fusion.1), channel_id=1, source_target_pairs={{0,2},{2,0},{4,6},{6,4},{8,10},{10,8},{12,14},{14,12},{16,18},{18,... | collective-permute-start | bytes 10223624 | tf_op jit(solution)/shard_map/ppermute | solution.py:55
  307.9 83.0 %collective-permute-start.62 = (bf16[8,64,3328]{2,1,0:T(8,128)(2,1)}, bf16[8,64,3328]{2,1,0:T(8,128)(2,1)}, u32[]{:S(2)}, u32[]{:S(2)}) collective-permute-start(bf16[8,64,3328]{2,1,0:T(8,128)(2,1)} %slice_bitcast_fusion), channel_id=1, source_target_pairs={{0,2},{2,0},{4,6},{6,4},{8,10},{10,8},{12,14},{14,12},{16,18},{18,... | collective-permute-start | bytes 10223624 | tf_op jit(solution)/shard_map/ppermute | solution.py:55
  319.0 45.6 %collective-permute-start.12 = (bf16[64,3328]{1,0:T(8,128)(2,1)}, bf16[64,3328]{1,0:T(8,128)(2,1)}, u32[]{:S(2)}, u32[]{:S(2)}) collective-permute-start(bf16[64,3328]{1,0:T(8,128)(2,1)} %fusion.38), channel_id=1, source_target_pairs={{0,8},{2,10},{8,16},{10,18},{16,24},{18,26},{24,28},{26,30},{28,20... | collective-permute-start | bytes 1277960 | tf_op jit(solution)/shard_map/ppermute | solution.py:52
  350.9 17.2 %collective-permute-start.29 = (bf16[64,3328]{1,0:T(8,128)(2,1)S(1)}, bf16[64,3328]{1,0:T(8,128)(2,1)S(1)}, u32[]{:S(2)}, u32[]{:S(2)}) collective-permute-start(bf16[64,3328]{1,0:T(8,128)(2,1)S(1)} %copy-done.18), channel_id=1, source_target_pairs={{0,4},{2,6},{8,0},{10,2},{16,8},{18,10},{24,16},{26,18},{28,24},{3... | collective-permute-start | bytes 1277960 | tf_op jit(solution)/shard_map/ppermute | solution.py:52
  366.5 18.6 %collective-permute-start.13 = (bf16[64,3328]{1,0:T(8,128)(2,1)S(1)}, bf16[64,3328]{1,0:T(8,128)(2,1)S(1)}, u32[]{:S(2)}, u32[]{:S(2)}) collective-permute-start(bf16[64,3328]{1,0:T(8,128)(2,1)S(1)} %fusion.37), channel_id=1, source_target_pairs={{0,8},{2,10},{8,16},{10,18},{16,24},{18,26},{24,28},{26,30},{28,20... | collective-permute-start | bytes 1277960 | tf_op jit(solution)/shard_map/ppermute | solution.py:52
  369.9 18.7 %collective-permute-start.30 = (bf16[64,3328]{1,0:T(8,128)(2,1)S(1)}, bf16[64,3328]{1,0:T(8,128)(2,1)S(1)}, u32[]{:S(2)}, u32[]{:S(2)}) collective-permute-start(bf16[64,3328]{1,0:T(8,128)(2,1)S(1)} %fusion.28), channel_id=1, source_target_pairs={{0,4},{2,6},{8,0},{10,2},{16,8},{18,10},{24,16},{26,18},{28,24},{3... | collective-permute-start | bytes 1277960 | tf_op jit(solution)/shard_map/ppermute | solution.py:52
  370.4 21.0 %collective-permute-start.46 = (bf16[64,3328]{1,0:T(8,128)(2,1)S(1)}, bf16[64,3328]{1,0:T(8,128)(2,1)S(1)}, u32[]{:S(2)}, u32[]{:S(2)}) collective-permute-start(bf16[64,3328]{1,0:T(8,128)(2,1)S(1)} %copy-done.17), channel_id=1, source_target_pairs={{0,8},{2,10},{8,16},{10,18},{16,24},{18,26},{24,28},{26,30},{28,20... | collective-permute-start | bytes 1277960 | tf_op jit(solution)/shard_map/ppermute | solution.py:52
  387.0 12.0 %collective-permute-start.14 = (bf16[64,3328]{1,0:T(8,128)(2,1)S(1)}, bf16[64,3328]{1,0:T(8,128)(2,1)S(1)}, u32[]{:S(2)}, u32[]{:S(2)}) collective-permute-start(bf16[64,3328]{1,0:T(8,128)(2,1)S(1)} %fusion.36), channel_id=1, source_target_pairs={{0,8},{2,10},{8,16},{10,18},{16,24},{18,26},{24,28},{26,30},{28,20... | collective-permute-start | bytes 1277960 | tf_op jit(solution)/shard_map/ppermute | solution.py:52
  390.4 12.8 %collective-permute-start.31 = (bf16[64,3328]{1,0:T(8,128)(2,1)S(1)}, bf16[64,3328]{1,0:T(8,128)(2,1)S(1)}, u32[]{:S(2)}, u32[]{:S(2)}) collective-permute-start(bf16[64,3328]{1,0:T(8,128)(2,1)S(1)} %fusion.27), channel_id=1, source_target_pairs={{0,4},{2,6},{8,0},{10,2},{16,8},{18,10},{24,16},{26,18},{28,24},{3... | collective-permute-start | bytes 1277960 | tf_op jit(solution)/shard_map/ppermute | solution.py:52
  390.9 21.4 %collective-permute-start.63 = (bf16[64,3328]{1,0:T(8,128)(2,1)S(1)}, bf16[64,3328]{1,0:T(8,128)(2,1)S(1)}, u32[]{:S(2)}, u32[]{:S(2)}) collective-permute-start(bf16[64,3328]{1,0:T(8,128)(2,1)S(1)} %fusion.11), channel_id=1, source_target_pairs={{0,4},{2,6},{8,0},{10,2},{16,8},{18,10},{24,16},{26,18},{28,24},{3... | collective-permute-start | bytes 1277960 | tf_op jit(solution)/shard_map/ppermute | solution.py:52
  393.3 21.5 %collective-permute-start.47 = (bf16[64,3328]{1,0:T(8,128)(2,1)S(1)}, bf16[64,3328]{1,0:T(8,128)(2,1)S(1)}, u32[]{:S(2)}, u32[]{:S(2)}) collective-permute-start(bf16[64,3328]{1,0:T(8,128)(2,1)S(1)} %fusion.19), channel_id=1, source_target_pairs={{0,8},{2,10},{8,16},{10,18},{16,24},{18,26},{24,28},{26,30},{28,20... | collective-permute-start | bytes 1277960 | tf_op jit(solution)/shard_map/ppermute | solution.py:52
  400.8 17.5 %collective-permute-start.15 = (bf16[64,3328]{1,0:T(8,128)(2,1)S(1)}, bf16[64,3328]{1,0:T(8,128)(2,1)S(1)}, u32[]{:S(2)}, u32[]{:S(2)}) collective-permute-start(bf16[64,3328]{1,0:T(8,128)(2,1)S(1)} %fusion.35), channel_id=1, source_target_pairs={{0,8},{2,10},{8,16},{10,18},{16,24},{18,26},{24,28},{26,30},{28,20... | collective-permute-start | bytes 1277960 | tf_op jit(solution)/shard_map/ppermute | solution.py:52
  405.0 27.7 %collective-permute-start.32 = (bf16[64,3328]{1,0:T(8,128)(2,1)S(1)}, bf16[64,3328]{1,0:T(8,128)(2,1)S(1)}, u32[]{:S(2)}, u32[]{:S(2)}) collective-permute-start(bf16[64,3328]{1,0:T(8,128)(2,1)S(1)} %fusion.26), channel_id=1, source_target_pairs={{0,4},{2,6},{8,0},{10,2},{16,8},{18,10},{24,16},{26,18},{28,24},{3... | collective-permute-start | bytes 1277960 | tf_op jit(solution)/shard_map/ppermute | solution.py:52
  414.2 18.5 %collective-permute-start.64 = (bf16[64,3328]{1,0:T(8,128)(2,1)S(1)}, bf16[64,3328]{1,0:T(8,128)(2,1)S(1)}, u32[]{:S(2)}, u32[]{:S(2)}) collective-permute-start(bf16[64,3328]{1,0:T(8,128)(2,1)S(1)} %fusion.10), channel_id=1, source_target_pairs={{0,4},{2,6},{8,0},{10,2},{16,8},{18,10},{24,16},{26,18},{28,24},{3... | collective-permute-start | bytes 1277960 | tf_op jit(solution)/shard_map/ppermute | solution.py:52
  416.7 16.0 %collective-permute-start.48 = (bf16[64,3328]{1,0:T(8,128)(2,1)S(1)}, bf16[64,3328]{1,0:T(8,128)(2,1)S(1)}, u32[]{:S(2)}, u32[]{:S(2)}) collective-permute-start(bf16[64,3328]{1,0:T(8,128)(2,1)S(1)} %fusion.18), channel_id=1, source_target_pairs={{0,8},{2,10},{8,16},{10,18},{16,24},{18,26},{24,28},{26,30},{28,20... | collective-permute-start | bytes 1277960 | tf_op jit(solution)/shard_map/ppermute | solution.py:52
  420.1 12.6 %collective-permute-start.16 = (bf16[64,3328]{1,0:T(8,128)(2,1)S(1)}, bf16[64,3328]{1,0:T(8,128)(2,1)S(1)}, u32[]{:S(2)}, u32[]{:S(2)}) collective-permute-start(bf16[64,3328]{1,0:T(8,128)(2,1)S(1)} %fusion.34), channel_id=1, source_target_pairs={{0,8},{2,10},{8,16},{10,18},{16,24},{18,26},{24,28},{26,30},{28,20... | collective-permute-start | bytes 1277960 | tf_op jit(solution)/shard_map/ppermute | solution.py:52
  (28 other events, 466.6 us)
